TPU v7x, 32 devices: a whole 2x2x4 slice. The times are simulated.
32 devices in a mesh: bulk: 4 (over y, x), grp: 8 (over z, core).
Axes of the slice: x: 2, y: 2, z: 4, core: 2. Of those that a mesh axis runs over, the one named last changes fastest.
Arguments:
- embeddings: bfloat16 [16384, 768], P(('bulk', 'grp')), may hold values from -6 to 6
- cluster_ids: int32 [16384, 1], P(('bulk', 'grp')), may hold values from 0 to 3; in each aligned block of 512 rows (0 to 511, 512 to 1023, ...) at most 192 rows name the same one
- row_order: int32 [16384], P(('bulk', 'grp')), may hold values from 0 to 16383, each once
Outputs:
- earlier_max: float32 [16384], P(('bulk', 'grp'))
Inputs may be any that keep to these rules, and one draw needn't show every extreme that they name: `cluster_ids`: the rows of one device name any one cluster at most 192 times; some cluster is named exactly 192 times by some device's rows.
All inputs are finite; a program needn't handle non-finite values.
Results may differ from a plain program's by a relative error of at most 0.0013.
Values may be sent and summed in bfloat16 or wider, within the bound.
No kernel may reach another device: no remote copies, remote signals or barrier semaphores. Data moves between devices by JAX's collectives and lax.ppermute only.
A program may use at most 64 MiB of HBM per device.

v0:
```python
import jax
import jax.numpy as jnp
from jax import lax
from jax.sharding import PartitionSpec as P


def on_device(embeddings, cluster_ids, row_order):
    rows = embeddings.shape[0]
    width = embeddings.shape[1]
    owners = lax.axis_size("bulk")
    capacity = 3 * rows // (2 * owners)
    values = embeddings.astype(jnp.float32)
    unit = (values * lax.rsqrt(jnp.sum(values * values, axis=1, keepdims=True) + 1e-06)).astype(
        jnp.bfloat16
    )
    target = cluster_ids[:, 0]
    onehot = (target[:, None] == jnp.arange(owners, dtype=jnp.int32)[None, :]).astype(jnp.int32)
    before = jnp.cumsum(onehot, axis=0) - onehot
    rank = jnp.sum(before * onehot, axis=1)
    slot = target * capacity + rank
    send_rows = jnp.zeros((owners * capacity, width), jnp.bfloat16).at[slot].set(unit)
    send_order = jnp.full((owners * capacity,), -1, jnp.int32).at[slot].set(row_order)
    recv_rows, recv_order = (
        lax.all_to_all(send_rows, "bulk", split_axis=0, concat_axis=0, tiled=True),
        lax.all_to_all(send_order, "bulk", split_axis=0, concat_axis=0, tiled=True),
    )
    initial = jnp.full((recv_rows.shape[0],), -1.0, jnp.float32)

    def fold_piece(best, piece):
        key_rows, key_order = piece
        scores = lax.dot_general(
            recv_rows, key_rows, (((1,), (1,)), ((), ())), preferred_element_type=jnp.float32
        )
        usable = (key_order[None, :] >= 0) & (key_order[None, :] < recv_order[:, None])
        return jnp.maximum(best, jnp.max(jnp.where(usable, scores, jnp.float32(-1.0)), axis=1))

    all_rows, all_order = (
        lax.all_gather(recv_rows, "grp", axis=0, tiled=True),
        lax.all_gather(recv_order, "grp", axis=0, tiled=True),
    )
    block = recv_rows.shape[0]
    pieces = all_rows.shape[0] // block

    def step_block(index, best):
        begin = index * block
        piece_rows = lax.dynamic_slice_in_dim(all_rows, begin, block, 0)
        piece_order = lax.dynamic_slice_in_dim(all_order, begin, block, 0)
        return fold_piece(best, (piece_rows, piece_order))

    best = lax.fori_loop(0, pieces, step_block, initial)
    returned = lax.all_to_all(best, "bulk", split_axis=0, concat_axis=0, tiled=True)
    return returned[slot]


def solution(mesh):
    return jax.shard_map(
        on_device,
        mesh=mesh,
        in_specs=(P(("bulk", "grp"), None), P(("bulk", "grp"), None), P(("bulk", "grp"))),
        out_specs=P(("bulk", "grp")),
        check_vma=False,
    )
```

profile of v0, /device:TPU:0, one launch (start us, length us, event | category | flops | bytes accessed | tf_op | source)
XLA Modules:
  0.0 169.5 jit_solution(2389378744590574773)
XLA Ops:
  6.5 0.7 fusion.12
  7.2 1.2 reduce-window.6
  8.4 0.2 slice_reduce_fusion
  8.6 0.2 reduce-window.9
  8.9 0.7 fusion.11
  9.6 0.7 compare_select_fusion
  10.3 1.4 fusion.3
  11.7 3.5 %scatter_custom_fusion.1 = bf16[768,768]{1,0:T(8,128)(2,1)S(1)} fusion(s32[512]{0:T(512)S(1)} %bitcast.41, bf16[512,768]{1,0:T(8,128)(2,1)} %param.5, f32[512]{0:T(512)S(1)} %add_rsqrt_fusion, bf16[]{:T(256)} %constant.56.clone.1), kind=kCustom, calls=%fused_computation.13 | custom fusion | flops 1179648 | bytes 1968130 | tf_op jit(solution)/shard_map/scatter | solution.py:21
  15.2 20.6 %all_to_all.38 = bf16[4,192,768]{2,1,0:T(8,128)(2,1)} all-to-all(bf16[4,192,768]{2,1,0:T(8,128)(2,1)S(1)} %bitcast.35), channel_id=1, replica_groups=mesh['bulk'=4,'grp'=8] {'bulk'}, dimensions={0} | all-to-all | bytes 2359296 | tf_op jit(solution)/shard_map/all_to_all | solution.py:24
  35.8 2.6 %scatter_custom_fusion = s32[768]{0:T(1024)S(1)} fusion(s32[512]{0:T(512)S(1)} %bitcast.42, s32[512]{0:T(512)} %param.7, s32[]{:T(128)} %constant.61.clone.1), kind=kCustom, calls=%fused_computation.28 | custom fusion | bytes 3584 | tf_op jit(solution)/shard_map/scatter | solution.py:22
  38.4 0.7 all_to_all.33
  39.1 3.2 %all-to-all-start = ((s32[4,192,1]{1,2,0:T(1,128)}), s32[4,192,1]{1,2,0:T(1,128)S(1)}, u32[]{:S(2)}, u32[]{:S(2)}) async-start(s32[4,192,1]{1,2,0:T(1,128)} %all_to_all.33), calls=%async_computation | async-start | bytes 8192 | tf_op jit(solution)/shard_map/all_to_all | solution.py:25
  42.4 4.6 %all-to-all-done = s32[4,192,1]{1,2,0:T(1,128)S(1)} async-done(((s32[4,192,1]{1,2,0:T(1,128)}), s32[4,192,1]{1,2,0:T(1,128)S(1)}, u32[]{:S(2)}, u32[]{:S(2)}) %all-to-all-start) | async-done | bytes 3104 | tf_op jit(solution)/shard_map/all_to_all | solution.py:25
  47.0 0.1 reshape.58
  47.2 15.3 %all-gather = s32[8,1,768]{2,1,0:T(1,128)S(1)} all-gather(s32[1,1,768]{2,1,0:T(1,128)S(1)} %reshape.58), channel_id=1, replica_groups=mesh['bulk'=4,'grp'=8] {'grp'}, dimensions={0}, use_global_device_ids=true | all-gather | bytes 27648 | tf_op jit(solution)/shard_map/all_gather | solution.py:39
  62.5 64.1 %all-gather.3.cloned.1.call-done = bf16[6144,768]{1,0:T(8,128)(2,1)} async-done(((bf16[768,768]{1,0:T(8,128)(2,1)}), bf16[6144,768]{1,0:T(8,128)(2,1)}) %all-gather.3.cloned.1.call-update) | async-done | bytes 9437200 | tf_op jit(solution)/shard_map/all_gather | solution.py:38
  126.6 23.6 %while.14 = (s32[]{:T(128)}, f32[768]{0:T(1024)S(1)}, s32[6144]{0:T(1024)S(1)}, s32[768]{0:T(1024)S(1)}, bf16[6144,768]{1,0:T(8,128)(2,1)}, /*index=5*/bf16[768,...) while((s32[]{:T(128)}, f32[768]{0:T(1024)S(1)}, s32[6144]{0:T(1024)S(1)}, ...), condition=%wide.region_8.9_spmd.clone, body=%wide.region_6.8_spmd.clone.sunk | while | flops 908330496 | bytes 2385573 | solution.py:50
  126.7 2.8 %fusion.21 = f32[768]{0:T(1024)S(1)} fusion(bf16[768,768]{1,0:T(8,128)(2,1)} %get-tuple-element.216, bf16[6144,768]{1,0:T(8,128)(2,1)} %get-tuple-element.215, s32[]{:T(128)S(6)} %select_n.32, s32[768]{0:T(1024)S(1)} %get-tuple-element.214, s32[768]{0:T(1024)S(1)} %get-tuple-element.189, pred[768]{0:T(1024)(128)(4,1)S(1)} %get-tuple-element.190), kind=kOutput, calls=%fused_computation.4.clone.1 | convolution fusion | flops 908328192 | bytes 2369284 | tf_op jit(solution)/shard_map/while/body/eval_jaxpr/dot_general | solution.py:31
  129.5 0.1 broadcast_compare_fusion.2
  129.6 2.8 %fusion.21 = f32[768]{0:T(1024)S(1)} fusion(bf16[768,768]{1,0:T(8,128)(2,1)} %get-tuple-element.216, bf16[6144,768]{1,0:T(8,128)(2,1)} %get-tuple-element.215, s32[]{:T(128)S(6)} %select_n.32, s32[768]{0:T(1024)S(1)} %get-tuple-element.214, s32[768]{0:T(1024)S(1)} %get-tuple-element.189, pred[768]{0:T(1024)(128)(4,1)S(1)} %get-tuple-element.190), kind=kOutput, calls=%fused_computation.4.clone.1 | convolution fusion | flops 908328192 | bytes 2369284 | tf_op jit(solution)/shard_map/while/body/eval_jaxpr/dot_general | solution.py:31
  132.5 0.1 broadcast_compare_fusion.2
  132.6 2.8 %fusion.21 = f32[768]{0:T(1024)S(1)} fusion(bf16[768,768]{1,0:T(8,128)(2,1)} %get-tuple-element.216, bf16[6144,768]{1,0:T(8,128)(2,1)} %get-tuple-element.215, s32[]{:T(128)S(6)} %select_n.32, s32[768]{0:T(1024)S(1)} %get-tuple-element.214, s32[768]{0:T(1024)S(1)} %get-tuple-element.189, pred[768]{0:T(1024)(128)(4,1)S(1)} %get-tuple-element.190), kind=kOutput, calls=%fused_computation.4.clone.1 | convolution fusion | flops 908328192 | bytes 2369284 | tf_op jit(solution)/shard_map/while/body/eval_jaxpr/dot_general | solution.py:31
  135.5 2.8 %fusion.21 = f32[768]{0:T(1024)S(1)} fusion(bf16[768,768]{1,0:T(8,128)(2,1)} %get-tuple-element.216, bf16[6144,768]{1,0:T(8,128)(2,1)} %get-tuple-element.215, s32[]{:T(128)S(6)} %select_n.32, s32[768]{0:T(1024)S(1)} %get-tuple-element.214, s32[768]{0:T(1024)S(1)} %get-tuple-element.189, pred[768]{0:T(1024)(128)(4,1)S(1)} %get-tuple-element.190), kind=kOutput, calls=%fused_computation.4.clone.1 | convolution fusion | flops 908328192 | bytes 2369284 | tf_op jit(solution)/shard_map/while/body/eval_jaxpr/dot_general | solution.py:31
  138.5 2.8 %fusion.21 = f32[768]{0:T(1024)S(1)} fusion(bf16[768,768]{1,0:T(8,128)(2,1)} %get-tuple-element.216, bf16[6144,768]{1,0:T(8,128)(2,1)} %get-tuple-element.215, s32[]{:T(128)S(6)} %select_n.32, s32[768]{0:T(1024)S(1)} %get-tuple-element.214, s32[768]{0:T(1024)S(1)} %get-tuple-element.189, pred[768]{0:T(1024)(128)(4,1)S(1)} %get-tuple-element.190), kind=kOutput, calls=%fused_computation.4.clone.1 | convolution fusion | flops 908328192 | bytes 2369284 | tf_op jit(solution)/shard_map/while/body/eval_jaxpr/dot_general | solution.py:31
  141.4 2.8 %fusion.21 = f32[768]{0:T(1024)S(1)} fusion(bf16[768,768]{1,0:T(8,128)(2,1)} %get-tuple-element.216, bf16[6144,768]{1,0:T(8,128)(2,1)} %get-tuple-element.215, s32[]{:T(128)S(6)} %select_n.32, s32[768]{0:T(1024)S(1)} %get-tuple-element.214, s32[768]{0:T(1024)S(1)} %get-tuple-element.189, pred[768]{0:T(1024)(128)(4,1)S(1)} %get-tuple-element.190), kind=kOutput, calls=%fused_computation.4.clone.1 | convolution fusion | flops 908328192 | bytes 2369284 | tf_op jit(solution)/shard_map/while/body/eval_jaxpr/dot_general | solution.py:31
  144.4 2.8 %fusion.21 = f32[768]{0:T(1024)S(1)} fusion(bf16[768,768]{1,0:T(8,128)(2,1)} %get-tuple-element.216, bf16[6144,768]{1,0:T(8,128)(2,1)} %get-tuple-element.215, s32[]{:T(128)S(6)} %select_n.32, s32[768]{0:T(1024)S(1)} %get-tuple-element.214, s32[768]{0:T(1024)S(1)} %get-tuple-element.189, pred[768]{0:T(1024)(128)(4,1)S(1)} %get-tuple-element.190), kind=kOutput, calls=%fused_computation.4.clone.1 | convolution fusion | flops 908328192 | bytes 2369284 | tf_op jit(solution)/shard_map/while/body/eval_jaxpr/dot_general | solution.py:31
  147.3 0.1 broadcast_compare_fusion.2
  147.3 2.8 %fusion.21 = f32[768]{0:T(1024)S(1)} fusion(bf16[768,768]{1,0:T(8,128)(2,1)} %get-tuple-element.216, bf16[6144,768]{1,0:T(8,128)(2,1)} %get-tuple-element.215, s32[]{:T(128)S(6)} %select_n.32, s32[768]{0:T(1024)S(1)} %get-tuple-element.214, s32[768]{0:T(1024)S(1)} %get-tuple-element.189, pred[768]{0:T(1024)(128)(4,1)S(1)} %get-tuple-element.190), kind=kOutput, calls=%fused_computation.4.clone.1 | convolution fusion | flops 908328192 | bytes 2369284 | tf_op jit(solution)/shard_map/while/body/eval_jaxpr/dot_general | solution.py:31
  150.2 0.7 all_to_all.34
  150.9 3.6 %all-to-all-start.2 = ((f32[4,192,1]{1,2,0:T(1,128)}), f32[4,192,1]{1,2,0:T(1,128)S(1)}, u32[]{:S(2)}, u32[]{:S(2)}) async-start(f32[4,192,1]{1,2,0:T(1,128)} %all_to_all.34), calls=%async_computation.2 | async-start | bytes 8192 | tf_op jit(solution)/shard_map/all_to_all | solution.py:51
  154.5 4.7 %all-to-all-done.2 = f32[4,192,1]{1,2,0:T(1,128)S(1)} async-done(((f32[4,192,1]{1,2,0:T(1,128)}), f32[4,192,1]{1,2,0:T(1,128)S(1)}, u32[]{:S(2)}, u32[]{:S(2)}) %all-to-all-start.2) | async-done | bytes 3104 | tf_op jit(solution)/shard_map/all_to_all | solution.py:51
  159.3 3.4 %gather_fusion = f32[512]{0:T(512)} fusion(f32[768]{0:T(1024)S(1)} %all_to_all.32, s32[1024]{0:T(1024)S(1)} %pad_clamp_fusion), kind=kCustom, calls=%fused_computation | custom fusion | bytes 6144 | tf_op jit(solution)/shard_map/gather | solution.py:52
  (23 shorter events, 0.8 us)
Async XLA Ops:
  6.5 120.1 %all-gather.3.cloned.1.call-start = ((), (), s32[]{:S(2)}) async-start(), calls=%async_computation.3 | async-start | bytes 10616832 | tf_op jit(solution)/shard_map/all_gather | solution.py:38
  39.1 7.9 %all-to-all-start = ((s32[4,192,1]{1,2,0:T(1,128)}), s32[4,192,1]{1,2,0:T(1,128)S(1)}, u32[]{:S(2)}, u32[]{:S(2)}) async-start(s32[4,192,1]{1,2,0:T(1,128)} %all_to_all.33), calls=%async_computation | async-start | bytes 8192 | tf_op jit(solution)/shard_map/all_to_all | solution.py:25
  150.9 8.3 %all-to-all-start.2 = ((f32[4,192,1]{1,2,0:T(1,128)}), f32[4,192,1]{1,2,0:T(1,128)S(1)}, u32[]{:S(2)}, u32[]{:S(2)}) async-start(f32[4,192,1]{1,2,0:T(1,128)} %all_to_all.34), calls=%async_computation.2 | async-start | bytes 8192 | tf_op jit(solution)/shard_map/all_to_all | solution.py:51
Sparse Core Ops, SparseCore 0:
  36.0 90.5 all-gather.2
where the time goes:
time: 170 us
  waiting for transfers between devices  73.4 us (43%)
  blocking collectives  35.9 us (21%)
  matrix products  22.6 us (13%)
  between operations  13.4 us (8%)
  other arithmetic  9.18 us (5%)
  local copies, waits for them, and re-layouts  7.81 us (5%)
  starting transfers between devices  6.85 us (4%)
    all_gather x1, waiting for transfers between devices, on_device(): lax.all_gather(recv_rows, 'grp', axis=0, tiled=True)  64.1 us
    dot_general x8, matrix products, fold_piece(): lax.dot_general(recv_rows, key_rows, (((1,), (1,)), ((), ())), preferred_...  22.6 us
    all_to_all x1, blocking collectives, on_device(): lax.all_to_all(send_rows, 'bulk', split_axis=0, concat_axis=0, tiled=True)  20.6 us
    all_gather x1, blocking collectives, on_device(): lax.all_gather(recv_order, 'grp', axis=0, tiled=True)  15.3 us
    all_to_all x1, waiting for transfers between devices, on_device(): lax.all_to_all(best, 'bulk', split_axis=0, concat_axis=0, tiled=True)  4.67 us
    all_to_all x1, waiting for transfers between devices, on_device(): lax.all_to_all(send_order, 'bulk', split_axis=0, concat_axis=0, tiled=True)  4.63 us
    all_to_all x1, starting transfers between devices, on_device(): lax.all_to_all(best, 'bulk', split_axis=0, concat_axis=0, tiled=True)  3.61 us
    scatter x1, other arithmetic, on_device(): jnp.zeros((owners * capacity, width), jnp.bfloat16).at[slot].set(unit)  3.52 us
  transfers between devices with their start and end apart: 3, of which 3 were waited for; matrix products, arithmetic and copies ran while one was open for 2% of the time, Pallas kernels for 0%

commit v1 on v0

v1 whole, which is shorter than its diff:
```python
import functools

import jax
import jax.numpy as jnp
from jax import lax
from jax.experimental import pallas as pl
from jax.experimental.pallas import tpu as pltpu
from jax.sharding import PartitionSpec as P

F32 = jnp.float32
BF16 = jnp.bfloat16
KEYS = 16
FRONT = 288
VMEM_LIMIT = 32 * 1024 * 1024


def plane_pairs(planes):
    load = {}
    sent, got = [0] * planes, [0] * planes

    def links(a, b):
        step = 1 if b > a else -1
        return [(p, p + step) for p in range(a, b, step)]

    chosen = []
    for distance in range(planes - 1, 0, -1):
        for low in range(planes - distance):
            options = []
            for a, b in ((low + distance, low), (low, low + distance)):
                path = links(a, b)
                worst = max(load.get(link, 0) for link in path)
                total = sum(load.get(link, 0) for link in path)
                options.append((worst, total, got[b], sent[a], len(options), a, b))
            a, b = min(options)[-2:]
            for link in links(a, b):
                load[link] = load.get(link, 0) + 1
            sent[a] += 1
            got[b] += 1
            chosen.append((a, b))
    rounds = []
    for a, b in chosen:
        for members in rounds:
            if all(a != c and b != d for c, d in members):
                members.append((a, b))
                break
        else:
            rounds.append([(a, b)])
    return rounds


def digits(ref, first):
    keys = ref[pl.ds(first, KEYS), :].astype(F32)
    order = keys[0:1] + 128.0 * keys[1:2] + 16384.0 * keys[2:3]
    return order, keys[3:4]


def columns(row, length):
    return jnp.transpose(jnp.broadcast_to(row, (8, row.shape[1])))[:length, 0:1]


def pack_kernel(values_ref, cluster_ref, order_ref, full_ref, *part_refs):
    rows, width = values_ref.shape
    fronts, backs = part_refs[0::2], part_refs[1::2]
    big = rows - backs[0].shape[0]
    order = order_ref[...]
    kept = [order & 127, (order >> 7) & 127, order >> 14, cluster_ref[...] + 1]
    kept += [jnp.zeros_like(order)] * (KEYS - len(kept))
    keys = jnp.concatenate(kept, axis=0).astype(F32).astype(BF16)
    if width > rows:
        keys = jnp.concatenate([keys, jnp.zeros((KEYS, width - rows), BF16)], axis=1)
    values = values_ref[...].astype(F32)
    unit = (values * lax.rsqrt(jnp.sum(values * values, axis=1, keepdims=True) + 1e-06)).astype(BF16)
    full_ref[0:rows, :] = unit
    full_ref[rows : rows + KEYS, :] = keys
    for front in fronts:
        front[0:big, :] = unit[:big]
        front[big : big + KEYS, :] = keys
    for back in backs:
        back[...] = unit[big:]


def pack(values, cluster, order, big, copies):
    rows, width = values.shape
    sizes = [rows + KEYS] + [big + KEYS, rows - big] * copies
    out = pl.pallas_call(
        pack_kernel,
        out_shape=[jax.ShapeDtypeStruct((size, width), BF16) for size in sizes],
        compiler_params=pltpu.CompilerParams(vmem_limit_bytes=VMEM_LIMIT),
        name="pack",
    )(values, cluster, order)
    return out[0], out[1::2], out[2::2]


def pair_kernel(plan, *refs):
    n_arrays, ms, ps, sides = plan
    arrays, best_ref, out_ref = refs[:n_arrays], refs[n_arrays], refs[n_arrays + 1]
    out_ref[...] = best_ref[...]
    keys = {}
    for _, _, _, keyed, first, _, _ in ms + ps:
        if (keyed, first) not in keys:
            keys[keyed, first] = digits(arrays[keyed], first)
    tiles = []
    for p, start, count, keyed, first, at, line in ps:
        order, cluster = keys[keyed, first]
        tile = min(256, count)
        for t in range(0, count, tile):
            span = slice(at + t, at + t + tile)
            rows = slice(start + t, start + t + tile)
            tiles.append([p, rows, tile, order[:, span], cluster[:, span], line, span, jnp.full((8, tile), -1.0, F32)])
    for (m, start, count, keyed, first, at, line), both in zip(ms, sides):
        order, cluster = (columns(row[:, at : at + count], count) for row in keys[keyed, first])
        m_rows = arrays[m][start : start + count, :]
        m_best = jnp.full((count, 128), -1.0, F32)
        for held in tiles:
            p, rows, tile, p_order, p_cluster, _, _, p_best = held
            scores = lax.dot_general(
                m_rows, arrays[p][rows, :], (((1,), (1,)), ((), ())), preferred_element_type=F32
            )
            scores = jnp.where(cluster == p_cluster, scores, -1.0)
            later = order > p_order
            mine = jnp.where(later, scores, -1.0)
            for c in range(0, tile, 128):
                m_best = jnp.maximum(m_best, mine[:, c : c + 128])
            if both:
                other = jnp.where(later, -1.0, scores).reshape(count // 8, 8, tile)
                held[-1] = jnp.maximum(p_best, jnp.max(other, axis=0))
        m_line = jnp.max(jnp.transpose(m_best), axis=0, keepdims=True)
        span = slice(at, at + count)
        out_ref[line : line + 1, span] = jnp.maximum(out_ref[line : line + 1, span], m_line)
    if any(sides):
        for *_, line, span, p_best in tiles:
            p_line = jnp.max(p_best, axis=0, keepdims=True)
            out_ref[line : line + 1, span] = jnp.maximum(out_ref[line : line + 1, span], p_line)


def fold(best, ms, ps, name):
    arrays = []

    def place(array):
        for at, held in enumerate(arrays):
            if held is array:
                return at
        arrays.append(array)
        return len(arrays) - 1

    def planned(piece):
        return place(piece[0]), *piece[1:3], place(piece[3]), *piece[4:7]

    plan = ([planned(piece) for piece in ms], [planned(piece) for piece in ps], [piece[-1] for piece in ms])
    return pl.pallas_call(
        functools.partial(pair_kernel, (len(arrays), *plan)),
        out_shape=jax.ShapeDtypeStruct(best.shape, F32),
        compiler_params=pltpu.CompilerParams(vmem_limit_bytes=VMEM_LIMIT),
        cost_estimate=pl.CostEstimate(flops=0, bytes_accessed=0, transcendentals=0),
        name=name,
    )(*arrays, best)


def after(x, *others):
    return lax.optimization_barrier((x, *others))[0]


def on_device(embeddings, cluster_ids, row_order):
    rows = embeddings.shape[0]
    n_bulk, n_grp = lax.axis_size("bulk"), lax.axis_size("grp")
    planes = n_grp // 2
    axes = ("bulk", "grp")

    def bulk_move(x, mask):
        pairs = [(b * n_grp + g, (b ^ mask) * n_grp + g) for b in range(n_bulk) for g in range(n_grp)]
        return lax.ppermute(x, axes, pairs)

    def core_move(x):
        pairs = [(b * n_grp + g, b * n_grp + (g ^ 1)) for b in range(n_bulk) for g in range(n_grp)]
        return lax.ppermute(x, axes, pairs)

    def plane_move(x, members):
        pairs = [
            (b * n_grp + 2 * s + c, b * n_grp + 2 * d + c) for b in range(n_bulk) for s, d in members for c in range(2)
        ]
        return lax.ppermute(x, axes, pairs)

    rounds = plane_pairs(planes)
    n_rounds = len(rounds)
    big = FRONT * rows // 512
    small = rows - big
    half = rows // 2
    last = n_bulk - 1
    full, fronts, backs = pack(embeddings, cluster_ids.reshape(1, rows), row_order.reshape(1, rows), big, n_rounds)

    own_lines = -(-(1 + n_rounds + n_bulk) // 8) * 8
    own_line, z_line = 0, lambda k: 1 + k
    p_line = lambda j: 1 + n_rounds + j
    t_line, tz_line = own_lines, lambda k: own_lines + 1 + k
    best = jnp.full((own_lines + -(-(1 + n_rounds) // 8) * 8, rows), -1.0, F32)

    def whole(x, line):
        return x, 0, rows, x, rows, 0, line

    twin = core_move(full)
    z_front = [plane_move(x, members) for x, members in zip(fronts, rounds)]
    bulk = [full] + [bulk_move(full, mask) for mask in range(1, last)]
    same = [whole(full, own_line) + (False,), whole(twin, t_line) + (False,)]
    blocks = [whole(bulk[j], p_line(j)) for j in range(last)]
    best = fold(best, same, blocks[:1], "own")
    d_top = bulk_move(bulk[1][:half], last ^ 1)
    d_end = bulk_move(bulk[last ^ 1][half:], 1)
    z_back = [plane_move(after(x, z_front[0], twin, *bulk[1:]), members) for x, members in zip(backs, rounds)]
    z_front_twin = core_move(jnp.concatenate([after(z_front[0], *bulk[1:])] + z_front[1:], axis=0))
    best = fold(best, same, blocks[1:], "plane")
    far = [(d_top, 0, half, d_end, half, 0, p_line(last)), (d_end, 0, half, d_end, half, half, p_line(last))]
    firsts, seconds = [], []
    for k in range(n_rounds):
        lead = k * (big + KEYS)
        firsts.append((z_front[k], 0, big, z_front[k], big, 0, z_line(k), True))
        firsts.append((z_front_twin, lead, big, z_front_twin, lead + big, 0, tz_line(k), True))
    best = fold(best, firsts, blocks, "front")
    best = fold(best, same + firsts, far, "far")
    z_back = [after(z_back[0], best)] + z_back[1:]
    z_back_twin = core_move(jnp.concatenate(z_back, axis=0))
    for k in range(n_rounds):
        lead = k * (big + KEYS)
        seconds.append((z_back[k], 0, small, z_front[k], big, big, z_line(k), True))
        seconds.append((z_back_twin, k * small, small, z_front_twin, lead + big, big, tz_line(k), True))
    best = fold(best, seconds, blocks + far, "back")

    from_twin = core_move(best[own_lines:])
    parts = [best[own_line], best[p_line(0)], from_twin[0]]
    parts += [bulk_move(best[p_line(j)], j) for j in range(1, n_bulk)]
    plane = lax.axis_index("grp") // 2
    for k, members in enumerate(rounds):
        total = jnp.maximum(best[z_line(k)], from_twin[1 + k])
        part = plane_move(total, [(d, s) for s, d in members])
        senders = [s for s, _ in members]
        if len(senders) < planes:
            sent = functools.reduce(jnp.logical_or, [plane == s for s in senders])
            part = jnp.where(sent, part, -1.0)
        parts.append(part)
    return functools.reduce(jnp.maximum, parts)


def solution(mesh):
    return jax.shard_map(
        on_device,
        mesh=mesh,
        in_specs=(P(("bulk", "grp"), None), P(("bulk", "grp"), None), P(("bulk", "grp"))),
        out_specs=P(("bulk", "grp")),
        check_vma=False,
    )
```

time: 170 us -> 70.1 us (0.41)
  waiting for transfers between devices: 73.4 us -> 24.1 us
  blocking collectives: 35.9 us -> 0 us
  matrix products: 22.6 us -> 0 us
  starting transfers between devices: 6.85 us -> 27.9 us
  Pallas kernels: 0 us -> 14.4 us
  between operations: 13.4 us -> 0.18 us
  other arithmetic: 9.18 us -> 0.71 us
  local copies, waits for them, and re-layouts: 7.81 us -> 2.56 us
    all_gather x1 -> x0, waiting for transfers between devices: 64.1 us -> none  [on_device(): lax.all_gather(recv_rows, 'grp', axis=0, tiled=True)]
    ppermute x0 -> x17, starting transfers between devices: none -> 27.9 us  [the longest x6 18.3 us: plane_move(): return lax.ppermute(x, axes, pairs)]
    ppermute x0 -> x17, waiting for transfers between devices: none -> 24.1 us  [the longest x6 18.3 us: plane_move(): return lax.ppermute(x, axes, pairs)]
    dot_general x8 -> x0, matrix products: 22.6 us -> none  [fold_piece(): lax.dot_general(recv_rows, key_rows, (((1,), (1,)), ((), ())), preferred_...]
    all_to_all x1 -> x0, blocking collectives: 20.6 us -> none  [on_device(): lax.all_to_all(send_rows, 'bulk', split_axis=0, concat_axis=0, tiled=True)]
    all_gather x1 -> x0, blocking collectives: 15.3 us -> none  [on_device(): lax.all_gather(recv_order, 'grp', axis=0, tiled=True)]
    pallas_call x0 -> x6, Pallas kernels: none -> 14.4 us  [the longest x5 14.1 us: fold(): pl.pallas_call(functools.partial(pair_kernel, (len(arrays), *plan)), out_...]
    all_to_all x2 -> x0, waiting for transfers between devices: 9.3 us -> none  [the longest x1 4.67 us: on_device(): lax.all_to_all(best, 'bulk', split_axis=0, concat_axis=0, tiled=True)]
  transfers between devices with their start and end apart: 3 -> 17, of which waited for: 3 -> 8; matrix products, arithmetic and copies ran while one was open for 2% -> 0% of each run, Pallas kernels for 0% -> 14%
where the time goes in v1:
time: 70.1 us; the launch traced here: 69.8 us
  starting transfers between devices  27.9 us (40%)
  waiting for transfers between devices  24.1 us (34%)
  Pallas kernels  14.4 us (21%)
  local copies, waits for them, and re-layouts  2.56 us (4%)
  other arithmetic  0.71 us (1%)
    ppermute x6, starting transfers between devices, plane_move(): return lax.ppermute(x, axes, pairs)  18.3 us
    ppermute x6, waiting for transfers between devices, plane_move(): return lax.ppermute(x, axes, pairs)  18.3 us
    pallas_call x5, Pallas kernels, fold(): pl.pallas_call(functools.partial(pair_kernel, (len(arrays), *plan)), out_...  14.1 us
    ppermute x7, starting transfers between devices, bulk_move(): return lax.ppermute(x, axes, pairs)  9.25 us
    ppermute x4, waiting for transfers between devices, core_move(): return lax.ppermute(x, axes, pairs)  3.2 us
    ppermute x7, waiting for transfers between devices, bulk_move(): return lax.ppermute(x, axes, pairs)  2.59 us
    unnamed x6, local copies, waits for them, and re-layouts  2.49 us
  transfers between devices with their start and end apart: 17, of which 8 were waited for; matrix products, arithmetic and copies ran while one was open for 0% of the time, Pallas kernels for 14%

profile of v1, /device:TPU:0, one launch (start us, length us, event | category | flops | bytes accessed | tf_op | source)
XLA Modules:
  0.0 69.8 jit_solution(4772190197620805304)
XLA Ops:
  0.0 1.1 %copy-done = bf16[512,768]{1,0:T(8,128)(2,1)S(1)} copy-done((bf16[512,768]{1,0:T(8,128)(2,1)S(1)}, bf16[512,768]{1,0:T(8,128)(2,1)}, u32[]{:S(2)}) %copy-start) | copy-done | bytes 786456
  1.1 0.7 copy-done.1
  1.8 0.7 copy-done.2
  2.5 0.3 pack.1
  2.8 3.0 %collective-permute-start.2 = (bf16[528,768]{1,0:T(8,128)(2,1)S(1)}, bf16[528,768]{1,0:T(8,128)(2,1)S(1)}, u32[]{:S(2)}, u32[]{:S(2)}) collective-permute-start(bf16[528,768]{1,0:T(8,128)(2,1)S(1)} %get-tuple-element.16.refs_0_.refs_3_.refs_6_), channel_id=1, source_target_pairs={{0,8},{1,9},{2,10},{3,11},{4,12},{5,13},{6,14},{7,15},{8,0},{9,1},... | collective-permute-start | bytes 2433032 | tf_op jit(solution)/shard_map/ppermute | solution.py:171
  5.8 1.5 %collective-permute-start.3 = (bf16[528,768]{1,0:T(8,128)(2,1)S(1)}, bf16[528,768]{1,0:T(8,128)(2,1)S(1)}, u32[]{:S(2)}, u32[]{:S(2)}) collective-permute-start(bf16[528,768]{1,0:T(8,128)(2,1)S(1)} %get-tuple-element.16.refs_0_.refs_3_.refs_6_), channel_id=1, source_target_pairs={{0,16},{1,17},{2,18},{3,19},{4,20},{5,21},{6,22},{7,23},{8,24},{9,... | collective-permute-start | bytes 2433032 | tf_op jit(solution)/shard_map/ppermute | solution.py:171
  7.3 2.6 %collective-permute-start = (bf16[304,768]{1,0:T(8,128)(2,1)S(1)}, bf16[304,768]{1,0:T(8,128)(2,1)S(1)}, u32[]{:S(2)}, u32[]{:S(2)}) collective-permute-start(bf16[304,768]{1,0:T(8,128)(2,1)S(1)} %get-tuple-element.15), channel_id=1, source_target_pairs={{6,0},{7,1},{0,4},{1,5},{2,6},{3,7},{4,2},{5,3},{14,8},{15,9},{8,1... | collective-permute-start | bytes 1400840 | tf_op jit(solution)/shard_map/ppermute | solution.py:181
  9.9 3.5 %collective-permute-start.5 = (bf16[304,768]{1,0:T(8,128)(2,1)S(1)}, bf16[304,768]{1,0:T(8,128)(2,1)S(1)}, u32[]{:S(2)}, u32[]{:S(2)}) collective-permute-start(bf16[304,768]{1,0:T(8,128)(2,1)S(1)} %get-tuple-element.19), channel_id=1, source_target_pairs={{0,2},{1,3},{6,4},{7,5},{8,10},{9,11},{14,12},{15,13},{16,18},{17,... | collective-permute-start | bytes 1400840 | tf_op jit(solution)/shard_map/ppermute | solution.py:181
  13.5 9.3 %collective-permute-done.refs_0_.refs_2_.refs_1_ = bf16[304,768]{1,0:T(8,128)(2,1)S(1)} collective-permute-done((bf16[304,768]{1,0:T(8,128)(2,1)S(1)}, bf16[304,768]{1,0:T(8,128)(2,1)S(1)}, u32[]{:S(2)}, u32[]{:S(2)}) %collective-permute-start) | collective-permute-done | bytes 466976 | tf_op jit(solution)/shard_map/ppermute | solution.py:181
  22.8 1.1 %collective-permute-done.2.refs_2_.refs_4_.refs_7_ = bf16[528,768]{1,0:T(8,128)(2,1)S(1)} collective-permute-done((bf16[528,768]{1,0:T(8,128)(2,1)S(1)}, bf16[528,768]{1,0:T(8,128)(2,1)S(1)}, u32[]{:S(2)}, u32[]{:S(2)}) %collective-permute-start.2) | collective-permute-done | bytes 811040 | tf_op jit(solution)/shard_map/ppermute | solution.py:171
  23.9 1.5 %collective-permute-done.3.refs_3_.refs_5_.refs_8_ = bf16[528,768]{1,0:T(8,128)(2,1)S(1)} collective-permute-done((bf16[528,768]{1,0:T(8,128)(2,1)S(1)}, bf16[528,768]{1,0:T(8,128)(2,1)S(1)}, u32[]{:S(2)}, u32[]{:S(2)}) %collective-permute-start.3) | collective-permute-done | bytes 811040 | tf_op jit(solution)/shard_map/ppermute | solution.py:171
  25.3 4.0 %collective-permute-done.5.refs_2_.refs_4_.refs_5_ = bf16[304,768]{1,0:T(8,128)(2,1)S(1)} collective-permute-done((bf16[304,768]{1,0:T(8,128)(2,1)S(1)}, bf16[304,768]{1,0:T(8,128)(2,1)S(1)}, u32[]{:S(2)}, u32[]{:S(2)}) %collective-permute-start.5) | collective-permute-done | bytes 466976 | tf_op jit(solution)/shard_map/ppermute | solution.py:181
  29.5 0.6 collective-permute-start.8
  30.2 0.6 collective-permute-start.7
  30.8 2.3 %collective-permute-start.4 = (bf16[224,768]{1,0:T(8,128)(2,1)S(1)}, bf16[224,768]{1,0:T(8,128)(2,1)S(1)}, u32[]{:S(2)}, u32[]{:S(2)}) collective-permute-start(bf16[224,768]{1,0:T(8,128)(2,1)S(1)} %get-tuple-element.17), channel_id=1, source_target_pairs={{6,0},{7,1},{0,4},{1,5},{2,6},{3,7},{4,2},{5,3},{14,8},{15,9},{8,1... | collective-permute-start | bytes 1032200 | tf_op jit(solution)/shard_map/ppermute | solution.py:181
  33.1 4.4 %collective-permute-start.9 = (bf16[224,768]{1,0:T(8,128)(2,1)S(1)}, bf16[224,768]{1,0:T(8,128)(2,1)S(1)}, u32[]{:S(2)}, u32[]{:S(2)}) collective-permute-start(bf16[224,768]{1,0:T(8,128)(2,1)S(1)} %get-tuple-element.22), channel_id=1, source_target_pairs={{0,2},{1,3},{6,4},{7,5},{8,10},{9,11},{14,12},{15,13},{16,18},{17,... | collective-permute-start | bytes 1032200 | tf_op jit(solution)/shard_map/ppermute | solution.py:181
  37.5 1.3 %own.1.refs_4_ = f32[16,512]{1,0:T(8,128)S(1)} custom-call(bf16[528,768]{1,0:T(8,128)(2,1)S(1)} %get-tuple-element.16.refs_0_.refs_3_.refs_6_, bf16[528,768]{1,0:T(8,128)(2,1)S(1)} %collective-permute-done.1.refs_1_, f32[16,512]{1,0:T(8,128)S(1)} %broadcast_in_dim.7.refs_2_), custom_call_target="tpu_custom_call" | custom-call | tf_op jit(solution)/shard_map/own/pallas_call | solution.py:150
  38.8 2.1 %plane.1.refs_6_ = f32[16,512]{1,0:T(8,128)S(1)} custom-call(bf16[528,768]{1,0:T(8,128)(2,1)S(1)} %get-tuple-element.16.refs_0_.refs_3_.refs_6_, bf16[528,768]{1,0:T(8,128)(2,1)S(1)} %collective-permute-done.1.refs_1_, bf16[528,768]{1,0:T(8,128)(2,1)S(1)} %collective-permute-done.2.refs_2_.refs_4_.refs_7_, ...), custom_call_target="tpu_custom_call" | custom-call | tf_op jit(solution)/shard_map/plane/pallas_call | solution.py:150
  41.0 3.5 %front.1.refs_7_ = f32[16,512]{1,0:T(8,128)S(1)} custom-call(bf16[304,768]{1,0:T(8,128)(2,1)S(1)} %collective-permute-done.refs_0_.refs_2_.refs_1_, bf16[608,768]{1,0:T(8,128)(2,1)S(1)} %collective-permute-done.6.refs_1_.refs_3_, bf16[304,768]{1,0:T(8,128)(2,1)S(1)} %collective-permute-done.5.refs_2_.refs_4_.refs_5_, ...), custom_call_target="tpu_custom_call" | custom-call | tf_op jit(solution)/shard_map/front/pallas_call | solution.py:150
  44.5 2.5 %far.1.refs_11_ = f32[16,512]{1,0:T(8,128)S(1)} custom-call(bf16[528,768]{1,0:T(8,128)(2,1)S(1)} %get-tuple-element.16.refs_0_.refs_3_.refs_6_, bf16[528,768]{1,0:T(8,128)(2,1)S(1)} %collective-permute-done.1.refs_1_, bf16[304,768]{1,0:T(8,128)(2,1)S(1)} %collective-permute-done.refs_0_.refs_2_.refs_1_, ...), custom_call_target="tpu_custom_call" | custom-call | tf_op jit(solution)/shard_map/far/pallas_call | solution.py:150
  47.0 0.9 %collective-permute-done.9.refs_4_ = bf16[224,768]{1,0:T(8,128)(2,1)S(1)} collective-permute-done((bf16[224,768]{1,0:T(8,128)(2,1)S(1)}, bf16[224,768]{1,0:T(8,128)(2,1)S(1)}, u32[]{:S(2)}, u32[]{:S(2)}) %collective-permute-start.9) | collective-permute-done | bytes 344096 | tf_op jit(solution)/shard_map/ppermute | solution.py:181
  48.0 2.1 %collective-permute-done.10.refs_2_ = bf16[448,768]{1,0:T(8,128)(2,1)S(1)} collective-permute-done((bf16[448,768]{1,0:T(8,128)(2,1)S(1)}, bf16[448,768]{1,0:T(8,128)(2,1)S(1)}, u32[]{:S(2)}, u32[]{:S(2)}) %collective-permute-start.10) | collective-permute-done | bytes 688160 | tf_op jit(solution)/shard_map/ppermute | solution.py:175
  50.2 4.6 %back.1 = f32[16,512]{1,0:T(8,128)S(1)} custom-call(bf16[224,768]{1,0:T(8,128)(2,1)S(1)} %collective-permute-done.4.refs_0_, bf16[304,768]{1,0:T(8,128)(2,1)S(1)} %collective-permute-done.refs_0_.refs_2_.refs_1_, bf16[448,768]{1,0:T(8,128)(2,1)S(1)} %collective-permute-done.10.refs_2_, bf16[608,768]{1,0:T(8,128)(2,1)S(1)} %collective-permute-done.6.refs_1_.refs_3_, ...), custom_call_target="tpu_custom_call" | custom-call | tf_op jit(solution)/shard_map/back/pallas_call | solution.py:150
  54.8 0.1 collective-permute-start.11
  54.9 1.1 %collective-permute-done.11 = f32[8,512]{1,0:T(8,128)S(1)} collective-permute-done((f32[8,512]{1,0:T(8,128)S(1)}, f32[8,512]{1,0:T(8,128)S(1)}, u32[]{:S(2)}, u32[]{:S(2)}) %collective-permute-start.11) | collective-permute-done | bytes 16416 | tf_op jit(solution)/shard_map/ppermute | solution.py:175
  56.0 1.6 %collective-permute-start.12 = (f32[512]{0:T(512)S(1)}, f32[512]{0:T(512)S(1)}, u32[]{:S(2)}, u32[]{:S(2)}) collective-permute-start(f32[512]{0:T(512)S(1)} %bitcast.15), channel_id=1, source_target_pairs={{0,8},{1,9},{2,10},{3,11},{4,12},{5,13},{6,14},{7,15},{8,0},{9,1},... | collective-permute-start | bytes 6152 | tf_op jit(solution)/shard_map/ppermute | solution.py:171
  57.6 1.5 %collective-permute-start.13 = (f32[512]{0:T(512)S(1)}, f32[512]{0:T(512)S(1)}, u32[]{:S(2)}, u32[]{:S(2)}) collective-permute-start(f32[512]{0:T(512)S(1)} %bitcast.14), channel_id=1, source_target_pairs={{0,16},{1,17},{2,18},{3,19},{4,20},{5,21},{6,22},{7,23},{8,24},{9,... | collective-permute-start | bytes 6152 | tf_op jit(solution)/shard_map/ppermute | solution.py:171
  59.1 0.5 collective-permute-start.14
  59.6 4.2 %collective-permute-start.15 = (f32[512]{0:T(512)S(1)}, f32[512]{0:T(512)S(1)}, u32[]{:S(2)}, u32[]{:S(2)}) collective-permute-start(f32[512]{0:T(512)S(1)} %bitcast.12), channel_id=1, source_target_pairs={{0,6},{1,7},{4,0},{5,1},{6,2},{7,3},{2,4},{3,5},{8,14},{9,15},{12,... | collective-permute-start | bytes 6152 | tf_op jit(solution)/shard_map/ppermute | solution.py:181
  63.8 1.3 %collective-permute-start.16 = (f32[512]{0:T(512)S(1)}, f32[512]{0:T(512)S(1)}, u32[]{:S(2)}, u32[]{:S(2)}) collective-permute-start(f32[512]{0:T(512)S(1)} %bitcast.11), channel_id=1, source_target_pairs={{2,0},{3,1},{4,6},{5,7},{10,8},{11,9},{12,14},{13,15},{18,16},{19,... | collective-permute-start | bytes 6152 | tf_op jit(solution)/shard_map/ppermute | solution.py:181
  65.1 4.1 %collective-permute-done.16 = f32[512]{0:T(512)S(1)} collective-permute-done((f32[512]{0:T(512)S(1)}, f32[512]{0:T(512)S(1)}, u32[]{:S(2)}, u32[]{:S(2)}) %collective-permute-start.16) | collective-permute-done | bytes 2080 | tf_op jit(solution)/shard_map/ppermute | solution.py:181
  69.3 0.6 select_maximum_fusion
  (22 shorter events, 0.4 us)
Async XLA Ops:
  0.0 1.1 %copy-start = (bf16[512,768]{1,0:T(8,128)(2,1)S(1)}, bf16[512,768]{1,0:T(8,128)(2,1)}, u32[]{:S(2)}) copy-start(bf16[512,768]{1,0:T(8,128)(2,1)} %values_ref.1) | copy-start | bytes 2359300
  1.1 0.7 copy-start.1
  1.8 0.7 copy-start.2
  2.8 21.1 %collective-permute-start.2 = (bf16[528,768]{1,0:T(8,128)(2,1)S(1)}, bf16[528,768]{1,0:T(8,128)(2,1)S(1)}, u32[]{:S(2)}, u32[]{:S(2)}) collective-permute-start(bf16[528,768]{1,0:T(8,128)(2,1)S(1)} %get-tuple-element.16.refs_0_.refs_3_.refs_6_), channel_id=1, source_target_pairs={{0,8},{1,9},{2,10},{3,11},{4,12},{5,13},{6,14},{7,15},{8,0},{9,1},... | collective-permute-start | bytes 2433032 | tf_op jit(solution)/shard_map/ppermute | solution.py:171
  5.8 19.5 %collective-permute-start.3 = (bf16[528,768]{1,0:T(8,128)(2,1)S(1)}, bf16[528,768]{1,0:T(8,128)(2,1)S(1)}, u32[]{:S(2)}, u32[]{:S(2)}) collective-permute-start(bf16[528,768]{1,0:T(8,128)(2,1)S(1)} %get-tuple-element.16.refs_0_.refs_3_.refs_6_), channel_id=1, source_target_pairs={{0,16},{1,17},{2,18},{3,19},{4,20},{5,21},{6,22},{7,23},{8,24},{9,... | collective-permute-start | bytes 2433032 | tf_op jit(solution)/shard_map/ppermute | solution.py:171
  7.3 15.4 %collective-permute-start = (bf16[304,768]{1,0:T(8,128)(2,1)S(1)}, bf16[304,768]{1,0:T(8,128)(2,1)S(1)}, u32[]{:S(2)}, u32[]{:S(2)}) collective-permute-start(bf16[304,768]{1,0:T(8,128)(2,1)S(1)} %get-tuple-element.15), channel_id=1, source_target_pairs={{6,0},{7,1},{0,4},{1,5},{2,6},{3,7},{4,2},{5,3},{14,8},{15,9},{8,1... | collective-permute-start | bytes 1400840 | tf_op jit(solution)/shard_map/ppermute | solution.py:181
  9.9 19.4 %collective-permute-start.5 = (bf16[304,768]{1,0:T(8,128)(2,1)S(1)}, bf16[304,768]{1,0:T(8,128)(2,1)S(1)}, u32[]{:S(2)}, u32[]{:S(2)}) collective-permute-start(bf16[304,768]{1,0:T(8,128)(2,1)S(1)} %get-tuple-element.19), channel_id=1, source_target_pairs={{0,2},{1,3},{6,4},{7,5},{8,10},{9,11},{14,12},{15,13},{16,18},{17,... | collective-permute-start | bytes 1400840 | tf_op jit(solution)/shard_map/ppermute | solution.py:181
  13.4 17.3 %collective-permute-start.1 = (bf16[528,768]{1,0:T(8,128)(2,1)S(1)}, bf16[528,768]{1,0:T(8,128)(2,1)S(1)}, u32[]{:S(2)}, u32[]{:S(2)}) collective-permute-start(bf16[528,768]{1,0:T(8,128)(2,1)S(1)} %get-tuple-element.16.refs_0_.refs_3_.refs_6_), channel_id=1, source_target_pairs={{0,1},{1,0},{2,3},{3,2},{4,5},{5,4},{6,7},{7,6},{8,9},{9,8},{10,11... | collective-permute-start | bytes 2433032 | tf_op jit(solution)/shard_map/ppermute | solution.py:175
  29.4 11.5 %collective-permute-start.6 = (bf16[608,768]{1,0:T(8,128)(2,1)S(1)}, bf16[608,768]{1,0:T(8,128)(2,1)S(1)}, u32[]{:S(2)}, u32[]{:S(2)}) collective-permute-start(bf16[608,768]{1,0:T(8,128)(2,1)S(1)} %pad_maximum_fusion), channel_id=1, source_target_pairs={{0,1},{1,0},{2,3},{3,2},{4,5},{5,4},{6,7},{7,6},{8,9},{9,8},{10,11... | collective-permute-start | bytes 2801672 | tf_op jit(solution)/shard_map/ppermute | solution.py:175
  29.5 15.0 %collective-permute-start.8 = (bf16[272,768]{1,0:T(8,128)(2,1)S(1)}, bf16[272,768]{1,0:T(8,128)(2,1)S(1)}, u32[]{:S(2)}, u32[]{:S(2)}) collective-permute-start(bf16[272,768]{1,0:T(8,128)(2,1)S(1)} %slice.53), channel_id=1, source_target_pairs={{0,8},{1,9},{2,10},{3,11},{4,12},{5,13},{6,14},{7,15},{8,0},{9,1},... | collective-permute-start | bytes 1253384 | tf_op jit(solution)/shard_map/ppermute | solution.py:171
  30.2 14.3 %collective-permute-start.7 = (bf16[256,768]{1,0:T(8,128)(2,1)S(1)}, bf16[256,768]{1,0:T(8,128)(2,1)S(1)}, u32[]{:S(2)}, u32[]{:S(2)}) collective-permute-start(bf16[256,768]{1,0:T(8,128)(2,1)S(1)} %slice.52), channel_id=1, source_target_pairs={{0,16},{1,17},{2,18},{3,19},{4,20},{5,21},{6,22},{7,23},{8,24},{9,... | collective-permute-start | bytes 1179656 | tf_op jit(solution)/shard_map/ppermute | solution.py:171
  30.8 16.2 %collective-permute-start.4 = (bf16[224,768]{1,0:T(8,128)(2,1)S(1)}, bf16[224,768]{1,0:T(8,128)(2,1)S(1)}, u32[]{:S(2)}, u32[]{:S(2)}) collective-permute-start(bf16[224,768]{1,0:T(8,128)(2,1)S(1)} %get-tuple-element.17), channel_id=1, source_target_pairs={{6,0},{7,1},{0,4},{1,5},{2,6},{3,7},{4,2},{5,3},{14,8},{15,9},{8,1... | collective-permute-start | bytes 1032200 | tf_op jit(solution)/shard_map/ppermute | solution.py:181
  33.1 14.8 %collective-permute-start.9 = (bf16[224,768]{1,0:T(8,128)(2,1)S(1)}, bf16[224,768]{1,0:T(8,128)(2,1)S(1)}, u32[]{:S(2)}, u32[]{:S(2)}) collective-permute-start(bf16[224,768]{1,0:T(8,128)(2,1)S(1)} %get-tuple-element.22), channel_id=1, source_target_pairs={{0,2},{1,3},{6,4},{7,5},{8,10},{9,11},{14,12},{15,13},{16,18},{17,... | collective-permute-start | bytes 1032200 | tf_op jit(solution)/shard_map/ppermute | solution.py:181
  48.0 2.2 %collective-permute-start.10 = (bf16[448,768]{1,0:T(8,128)(2,1)S(1)}, bf16[448,768]{1,0:T(8,128)(2,1)S(1)}, u32[]{:S(2)}, u32[]{:S(2)}) collective-permute-start(bf16[448,768]{1,0:T(8,128)(2,1)S(1)} %pad_maximum_fusion.1), channel_id=1, source_target_pairs={{0,1},{1,0},{2,3},{3,2},{4,5},{5,4},{6,7},{7,6},{8,9},{9,8},{10,11... | collective-permute-start | bytes 2064392 | tf_op jit(solution)/shard_map/ppermute | solution.py:175
  54.8 1.2 %collective-permute-start.11 = (f32[8,512]{1,0:T(8,128)S(1)}, f32[8,512]{1,0:T(8,128)S(1)}, u32[]{:S(2)}, u32[]{:S(2)}) collective-permute-start(f32[8,512]{1,0:T(8,128)S(1)} %slice.56), channel_id=1, source_target_pairs={{0,1},{1,0},{2,3},{3,2},{4,5},{5,4},{6,7},{7,6},{8,9},{9,8},{10,11... | collective-permute-start | bytes 49160 | tf_op jit(solution)/shard_map/ppermute | solution.py:175
  56.0 9.1 %collective-permute-start.12 = (f32[512]{0:T(512)S(1)}, f32[512]{0:T(512)S(1)}, u32[]{:S(2)}, u32[]{:S(2)}) collective-permute-start(f32[512]{0:T(512)S(1)} %bitcast.15), channel_id=1, source_target_pairs={{0,8},{1,9},{2,10},{3,11},{4,12},{5,13},{6,14},{7,15},{8,0},{9,1},... | collective-permute-start | bytes 6152 | tf_op jit(solution)/shard_map/ppermute | solution.py:171
  57.6 7.6 %collective-permute-start.13 = (f32[512]{0:T(512)S(1)}, f32[512]{0:T(512)S(1)}, u32[]{:S(2)}, u32[]{:S(2)}) collective-permute-start(f32[512]{0:T(512)S(1)} %bitcast.14), channel_id=1, source_target_pairs={{0,16},{1,17},{2,18},{3,19},{4,20},{5,21},{6,22},{7,23},{8,24},{9,... | collective-permute-start | bytes 6152 | tf_op jit(solution)/shard_map/ppermute | solution.py:171
  59.1 6.0 %collective-permute-start.14 = (f32[512]{0:T(512)S(1)}, f32[512]{0:T(512)S(1)}, u32[]{:S(2)}, u32[]{:S(2)}) collective-permute-start(f32[512]{0:T(512)S(1)} %bitcast.13), channel_id=1, source_target_pairs={{0,24},{1,25},{2,26},{3,27},{4,28},{5,29},{6,30},{7,31},{8,16},{9,... | collective-permute-start | bytes 6152 | tf_op jit(solution)/shard_map/ppermute | solution.py:171
  59.6 5.6 %collective-permute-start.15 = (f32[512]{0:T(512)S(1)}, f32[512]{0:T(512)S(1)}, u32[]{:S(2)}, u32[]{:S(2)}) collective-permute-start(f32[512]{0:T(512)S(1)} %bitcast.12), channel_id=1, source_target_pairs={{0,6},{1,7},{4,0},{5,1},{6,2},{7,3},{2,4},{3,5},{8,14},{9,15},{12,... | collective-permute-start | bytes 6152 | tf_op jit(solution)/shard_map/ppermute | solution.py:181
  63.8 5.5 %collective-permute-start.16 = (f32[512]{0:T(512)S(1)}, f32[512]{0:T(512)S(1)}, u32[]{:S(2)}, u32[]{:S(2)}) collective-permute-start(f32[512]{0:T(512)S(1)} %bitcast.11), channel_id=1, source_target_pairs={{2,0},{3,1},{4,6},{5,7},{10,8},{11,9},{12,14},{13,15},{18,16},{19,... | collective-permute-start | bytes 6152 | tf_op jit(solution)/shard_map/ppermute | solution.py:181

commit v2 on v1

v2 whole, which is shorter than its diff:
```python
import functools

import jax
import jax.numpy as jnp
from jax import lax
from jax.experimental import pallas as pl
from jax.experimental.pallas import tpu as pltpu
from jax.sharding import PartitionSpec as P

F32 = jnp.float32
BF16 = jnp.bfloat16
KEYS = 16
VMEM_LIMIT = 32 * 1024 * 1024


def plane_rounds(planes):
    rounds = [[(z, (z - k) % planes) for z in range(planes)] for k in range(1, (planes + 1) // 2)]
    if planes % 2 == 0:
        half = planes // 2
        rounds.append([(z, z + half) if z % 2 == 0 else (z + half, z) for z in range(half)])
    return rounds


def digits(ref, first):
    keys = ref[pl.ds(first, KEYS), :].astype(F32)
    order = keys[0:1] + 128.0 * keys[1:2] + 16384.0 * keys[2:3]
    return order, keys[3:4]


def columns(row, length):
    return jnp.transpose(jnp.broadcast_to(row, (8, row.shape[1])))[:length, 0:1]


def pack_kernel(values_ref, marks_ref, full_ref):
    rows, width = values_ref.shape
    values = values_ref[...].astype(F32)
    unit = values * lax.rsqrt(jnp.sum(values * values, axis=1, keepdims=True) + 1e-06)
    full_ref[0:rows, :] = unit.astype(BF16)
    order, cluster = marks_ref[0:1, :], marks_ref[1:2, :]
    kept = [order & 127, (order >> 7) & 127, order >> 14, cluster + 1]
    kept += [jnp.zeros_like(order)] * (KEYS - len(kept))
    keys = jnp.concatenate(kept, axis=0).astype(F32).astype(BF16)
    if width > rows:
        keys = jnp.concatenate([keys, jnp.zeros((KEYS, width - rows), BF16)], axis=1)
    full_ref[rows : rows + KEYS, :] = keys


def pack(values, marks):
    rows, width = values.shape
    return pl.pallas_call(
        pack_kernel,
        out_shape=jax.ShapeDtypeStruct((rows + KEYS, width), BF16),
        compiler_params=pltpu.CompilerParams(vmem_limit_bytes=VMEM_LIMIT),
        name="pack",
    )(values, marks)


def row_range(arrays, parts, low, count):
    taken = []
    for array, first, rows in parts:
        begin, end = max(low, 0), min(low + count, rows)
        if begin < end:
            taken.append((array, slice(first + begin, first + end)))
        low -= rows

    def read():
        held = [arrays[array][rows, :] for array, rows in taken]
        return held[0] if len(held) == 1 else jnp.concatenate(held, axis=0)

    return read


def pair_kernel(plan, *refs):
    n_arrays, ms, ps, sides = plan
    arrays, best_ref, out_ref = refs[:n_arrays], refs[n_arrays], refs[n_arrays + 1]
    out_ref[...] = best_ref[...]
    keys = {}
    for keyed, first in [piece[3:5] for piece in ms] + [block[1:3] for block in ps]:
        if (keyed, first) not in keys:
            keys[keyed, first] = digits(arrays[keyed], first)
    tiles = []
    for parts, keyed, first, line in ps:
        order, cluster = keys[keyed, first]
        rows = sum(count for _, _, count in parts)
        tile = min(256, rows)
        for low in range(0, rows, tile):
            span = slice(low, low + tile)
            tiles.append([row_range(arrays, parts, low, tile), order[:, span], cluster[:, span], line, span, tile])
            tiles[-1].append(jnp.full((8, tile), -1.0, F32))
    for (m, start, count, keyed, first, at, line), both in zip(ms, sides):
        order, cluster = (columns(row[:, at : at + count], count) for row in keys[keyed, first])
        m_rows = arrays[m][start : start + count, :]
        m_best = jnp.full((count, 128), -1.0, F32)
        for held in tiles:
            p_rows, p_order, p_cluster, _, _, tile, p_best = held
            scores = lax.dot_general(m_rows, p_rows(), (((1,), (1,)), ((), ())), preferred_element_type=F32)
            scores = jnp.where(cluster == p_cluster, scores, -1.0)
            later = order > p_order
            mine = jnp.where(later, scores, -1.0)
            for c in range(0, tile, 128):
                m_best = jnp.maximum(m_best, mine[:, c : c + 128])
            if both:
                other = jnp.where(later, -1.0, scores).reshape(count // 8, 8, tile)
                held[-1] = jnp.maximum(p_best, jnp.max(other, axis=0))
        m_line = jnp.max(jnp.transpose(m_best), axis=0, keepdims=True)
        span = slice(at, at + count)
        out_ref[line : line + 1, span] = jnp.maximum(out_ref[line : line + 1, span], m_line)
    if any(sides):
        for _, _, _, line, span, _, p_best in tiles:
            p_line = jnp.max(p_best, axis=0, keepdims=True)
            out_ref[line : line + 1, span] = jnp.maximum(out_ref[line : line + 1, span], p_line)


def fold(best, ms, ps, name):
    arrays = []

    def place(array):
        for at, held in enumerate(arrays):
            if held is array:
                return at
        arrays.append(array)
        return len(arrays) - 1

    m_plan = [(place(m[0]), *m[1:3], place(m[3]), *m[4:7]) for m in ms]
    p_plan = [([(place(a), *rest) for a, *rest in p[0]], place(p[1]), *p[2:]) for p in ps]
    plan = (m_plan, p_plan, [m[-1] for m in ms])
    return pl.pallas_call(
        functools.partial(pair_kernel, (len(arrays), *plan)),
        out_shape=jax.ShapeDtypeStruct(best.shape, F32),
        compiler_params=pltpu.CompilerParams(vmem_limit_bytes=VMEM_LIMIT),
        cost_estimate=pl.CostEstimate(flops=0, bytes_accessed=0, transcendentals=0),
        name=name,
    )(*arrays, best)


def after(x, *others):
    return lax.optimization_barrier((x, *others))[0]


def on_device(embeddings, cluster_ids, row_order):
    rows = embeddings.shape[0]
    n_bulk, n_grp = lax.axis_size("bulk"), lax.axis_size("grp")
    planes = n_grp // 2
    axes = ("bulk", "grp")

    def bulk_move(x, mask):
        pairs = [(b * n_grp + g, (b ^ mask) * n_grp + g) for b in range(n_bulk) for g in range(n_grp)]
        return lax.ppermute(x, axes, pairs)

    def core_move(x):
        pairs = [(b * n_grp + g, b * n_grp + (g ^ 1)) for b in range(n_bulk) for g in range(n_grp)]
        return lax.ppermute(x, axes, pairs)

    def plane_move(x, members):
        pairs = [
            (b * n_grp + 2 * s + c, b * n_grp + 2 * d + c) for b in range(n_bulk) for s, d in members for c in range(2)
        ]
        return lax.ppermute(x, axes, pairs)

    rounds = plane_rounds(planes)
    n_rounds = len(rounds)
    half, near_cut = rows // 2, 5 * rows // 8
    last = n_bulk - 1
    full = pack(embeddings, jnp.stack([row_order, cluster_ids.reshape(rows)]))

    own_line, t_line = 0, 1
    z_line, tz_line = lambda k: 2 + 2 * k, lambda k: 3 + 2 * k
    p_line = lambda j: 2 + 2 * n_rounds + j
    best = jnp.full((-(-p_line(n_bulk) // 8) * 8, rows), -1.0, F32)

    def whole(x, line, both):
        return x, 0, rows, x, rows, 0, line, both

    def block(x, line):
        return [(x, 0, rows)], x, rows, line

    def go_home(lines, k):
        back = {(d, s) for s, d in rounds[k]}
        if len(back) < planes:
            back |= {(s, d) for d, s in back}
        return plane_move(lines, sorted(back))

    twin = core_move(full)
    z = [plane_move(full, members) for members in rounds]
    bulk = [bulk_move(full, mask) for mask in range(1, last)]
    same = [whole(full, own_line, False), whole(twin, t_line, False)]
    blocks = [block(full, p_line(0))]
    best = fold(best, same, blocks, "own")
    bulk = [full] + [after(x, best) for x in bulk]
    d_top = bulk_move(bulk[1][:near_cut], last ^ 1)
    d_end = bulk_move(bulk[last ^ 1][near_cut:], 1)
    k = n_rounds - 1
    z_twin = [(core_move(x[:half]), core_move(x[half:])) for x in z[:k]]
    near = [block(bulk[j], p_line(j)) for j in range(1, last)]
    far = [([(d_top, 0, near_cut), (d_end, 0, rows - near_cut)], d_end, rows - near_cut, p_line(last))]
    most = []
    for r in range(k):
        top, end = z_twin[r]
        most.append(whole(z[r], z_line(r), True))
        most.append((end, 0, half, end, half, half, tz_line(r), True))
        most.append((top, 0, half, end, half, 0, tz_line(r), True))
    best = fold(best, same, near, "near")
    best = fold(best, most, blocks + near, "column")
    best = fold(best, same + most, far, "far")

    parts = [go_home(best[z_line(r) : tz_line(r) + 1], r) for r in range(k)]
    blocks += near + far
    z_last = after(z[k], best)
    z_top, z_end = core_move(z_last[:half]), core_move(z_last[half:])
    best = fold(best, [whole(z_last, z_line(k), True)], blocks, "last")
    best = fold(best, [(z_end, 0, half, z_end, half, half, tz_line(k), True)], blocks, "end")
    parts = [after(x, best) for x in parts]
    best = fold(after(best, *parts), [(z_top, 0, half, z_end, half, 0, tz_line(k), True)], blocks, "top")

    parts.append(go_home(best[z_line(k) : tz_line(k) + 1], k))
    both = functools.reduce(jnp.maximum, parts, best[own_line : t_line + 1])
    mine = best[p_line(0)]
    for j in range(1, n_bulk):
        mine = jnp.maximum(mine, bulk_move(best[p_line(j)], j))
    return jnp.maximum(jnp.maximum(both[0], core_move(both[1])), mine)


def solution(mesh):
    return jax.shard_map(
        on_device,
        mesh=mesh,
        in_specs=(P(("bulk", "grp"), None), P(("bulk", "grp"), None), P(("bulk", "grp"))),
        out_specs=P(("bulk", "grp")),
        check_vma=False,
    )
```

time: 70.1 us -> 60.9 us (0.87)
  starting transfers between devices: 27.9 us -> 20 us
    ppermute x7, waiting for transfers between devices: 2.59 us -> 19 us  [bulk_move(): return lax.ppermute(x, axes, pairs)]
    ppermute x6 -> x4, waiting for transfers between devices: 18.3 us -> 4.39 us  [plane_move(): return lax.ppermute(x, axes, pairs)]
    ppermute x6 -> x4, starting transfers between devices: 18.3 us -> 8.1 us  [plane_move(): return lax.ppermute(x, axes, pairs)]
    ppermute x4 -> x6, waiting for transfers between devices: 3.2 us -> 0.02 us  [core_move(): return lax.ppermute(x, axes, pairs)]
    ppermute x4 -> x6, starting transfers between devices: 0.34 us -> 1.84 us  [core_move(): return lax.ppermute(x, axes, pairs)]
    ppermute x7, starting transfers between devices: 9.25 us -> 10.1 us  [bulk_move(): return lax.ppermute(x, axes, pairs)]
    unnamed x6 -> x4, local copies, waits for them, and re-layouts: 2.49 us -> 1.81 us
    pallas_call x5 -> x7, Pallas kernels: 14.1 us -> 13.5 us  [fold(): pl.pallas_call(functools.partial(pair_kernel, (len(arrays), *plan)), out_...]
  transfers between devices with their start and end apart: 17 -> 17, of which waited for: 8 -> 9; matrix products, arithmetic and copies ran while one was open for 0% -> 0% of each run, Pallas kernels for 14% -> 20%
where the time goes in v2:
time: 60.9 us; the launch traced here: 60.7 us
  waiting for transfers between devices  23.4 us (38%)
  starting transfers between devices  20 us (33%)
  Pallas kernels  13.8 us (23%)
  local copies, waits for them, and re-layouts  2 us (3%)
  other arithmetic  1.28 us (2%)
    ppermute x7, waiting for transfers between devices, bulk_move(): return lax.ppermute(x, axes, pairs)  19 us
    pallas_call x7, Pallas kernels, fold(): pl.pallas_call(functools.partial(pair_kernel, (len(arrays), *plan)), out_...  13.5 us
    ppermute x7, starting transfers between devices, bulk_move(): return lax.ppermute(x, axes, pairs)  10.1 us
    ppermute x4, starting transfers between devices, plane_move(): return lax.ppermute(x, axes, pairs)  8.1 us
    ppermute x4, waiting for transfers between devices, plane_move(): return lax.ppermute(x, axes, pairs)  4.39 us
    ppermute x6, starting transfers between devices, core_move(): return lax.ppermute(x, axes, pairs)  1.84 us
    unnamed x4, local copies, waits for them, and re-layouts  1.81 us
  transfers between devices with their start and end apart: 17, of which 9 were waited for; matrix products, arithmetic and copies ran while one was open for 0% of the time, Pallas kernels for 20%

profile of v2, /device:TPU:0, one launch (start us, length us, event | category | flops | bytes accessed | tf_op | source)
XLA Modules:
  0.0 60.7 jit_solution(2422476687654851936)
XLA Ops:
  0.0 0.7 %copy-done.1 = s32[512,1]{0,1:T(1,128)S(1)} copy-done((s32[512,1]{0,1:T(1,128)S(1)}, s32[512,1]{0,1:T(1,128)}, u32[]{:S(2)}) %copy-start.1) | copy-done | bytes 2072
  0.7 0.7 %pad_add_fusion.marks_ref = s32[2,512]{1,0:T(2,128)S(1)} fusion(s32[1,512]{1,0:T(1,128)S(1)} %bitcast.10, s32[1,512]{1,0:T(1,128)} %bitcast.11), kind=kLoop, calls=%fused_computation.2 | loop fusion | flops 1024 | bytes 8192 | tf_op jit(solution)/shard_map/stack | solution.py:164
  1.4 1.1 %copy-done = bf16[512,768]{1,0:T(8,128)(2,1)S(1)} copy-done((bf16[512,768]{1,0:T(8,128)(2,1)S(1)}, bf16[512,768]{1,0:T(8,128)(2,1)}, u32[]{:S(2)}) %copy-start) | copy-done | bytes 786456
  3.3 2.6 %collective-permute-start.5 = (bf16[528,768]{1,0:T(8,128)(2,1)S(1)}, bf16[528,768]{1,0:T(8,128)(2,1)S(1)}, u32[]{:S(2)}, u32[]{:S(2)}) collective-permute-start(bf16[528,768]{1,0:T(8,128)(2,1)S(1)} %pack.1.refs_0_.refs_3_.refs_1_.refs_2_), channel_id=1, source_target_pairs={{0,8},{1,9},{2,10},{3,11},{4,12},{5,13},{6,14},{7,15},{8,0},{9,1},... | collective-permute-start | bytes 2433032 | tf_op jit(solution)/shard_map/ppermute | solution.py:148
  5.8 3.6 %collective-permute-start.2 = (bf16[528,768]{1,0:T(8,128)(2,1)S(1)}, bf16[528,768]{1,0:T(8,128)(2,1)S(1)}, u32[]{:S(2)}, u32[]{:S(2)}) collective-permute-start(bf16[528,768]{1,0:T(8,128)(2,1)S(1)} %pack.1.refs_0_.refs_3_.refs_1_.refs_2_), channel_id=1, source_target_pairs={{0,6},{1,7},{2,0},{3,1},{4,2},{5,3},{6,4},{7,5},{8,14},{9,15},{10,... | collective-permute-start | bytes 2433032 | tf_op jit(solution)/shard_map/ppermute | solution.py:158
  9.4 1.5 %collective-permute-start.7 = (bf16[528,768]{1,0:T(8,128)(2,1)S(1)}, bf16[528,768]{1,0:T(8,128)(2,1)S(1)}, u32[]{:S(2)}, u32[]{:S(2)}) collective-permute-start(bf16[528,768]{1,0:T(8,128)(2,1)S(1)} %pack.1.refs_0_.refs_3_.refs_1_.refs_2_), channel_id=1, source_target_pairs={{0,16},{1,17},{2,18},{3,19},{4,20},{5,21},{6,22},{7,23},{8,24},{9,... | collective-permute-start | bytes 2433032 | tf_op jit(solution)/shard_map/ppermute | solution.py:148
  11.0 1.4 %collective-permute-start = (bf16[528,768]{1,0:T(8,128)(2,1)S(1)}, bf16[528,768]{1,0:T(8,128)(2,1)S(1)}, u32[]{:S(2)}, u32[]{:S(2)}) collective-permute-start(bf16[528,768]{1,0:T(8,128)(2,1)S(1)} %pack.1.refs_0_.refs_3_.refs_1_.refs_2_), channel_id=1, source_target_pairs={{0,4},{1,5},{6,2},{7,3},{8,12},{9,13},{14,10},{15,11},{16,20},{17,... | collective-permute-start | bytes 2433032 | tf_op jit(solution)/shard_map/ppermute | solution.py:158
  12.4 1.3 %own.1.refs_4_ = f32[16,512]{1,0:T(8,128)S(1)} custom-call(bf16[528,768]{1,0:T(8,128)(2,1)S(1)} %pack.1.refs_0_.refs_3_.refs_1_.refs_2_, bf16[528,768]{1,0:T(8,128)(2,1)S(1)} %collective-permute-done.1.refs_1_, f32[16,512]{1,0:T(8,128)S(1)} %broadcast_in_dim.3.refs_2_), custom_call_target="tpu_custom_call" | custom-call | tf_op jit(solution)/shard_map/own/pallas_call | solution.py:127
  13.7 10.8 %collective-permute-done.5.refs_2_.refs_4_.refs_3_ = bf16[528,768]{1,0:T(8,128)(2,1)S(1)} collective-permute-done((bf16[528,768]{1,0:T(8,128)(2,1)S(1)}, bf16[528,768]{1,0:T(8,128)(2,1)S(1)}, u32[]{:S(2)}, u32[]{:S(2)}) %collective-permute-start.5) | collective-permute-done | bytes 811040 | tf_op jit(solution)/shard_map/ppermute | solution.py:148
  24.5 1.9 %collective-permute-start.6 = (bf16[320,768]{1,0:T(8,128)(2,1)S(1)}, bf16[320,768]{1,0:T(8,128)(2,1)S(1)}, u32[]{:S(2)}, u32[]{:S(2)}) collective-permute-start(bf16[320,768]{1,0:T(8,128)(2,1)S(1)} %slice.47), channel_id=1, source_target_pairs={{0,16},{1,17},{2,18},{3,19},{4,20},{5,21},{6,22},{7,23},{8,24},{9,... | collective-permute-start | bytes 1474568 | tf_op jit(solution)/shard_map/ppermute | solution.py:148
  26.4 1.5 %collective-permute-done.2.refs_0_.refs_2_ = bf16[528,768]{1,0:T(8,128)(2,1)S(1)} collective-permute-done((bf16[528,768]{1,0:T(8,128)(2,1)S(1)}, bf16[528,768]{1,0:T(8,128)(2,1)S(1)}, u32[]{:S(2)}, u32[]{:S(2)}) %collective-permute-start.2) | collective-permute-done | bytes 811040 | tf_op jit(solution)/shard_map/ppermute | solution.py:158
  28.0 0.6 collective-permute-start.4
  28.6 1.8 %collective-permute-done.7.refs_3_.refs_5_.refs_4_ = bf16[528,768]{1,0:T(8,128)(2,1)S(1)} collective-permute-done((bf16[528,768]{1,0:T(8,128)(2,1)S(1)}, bf16[528,768]{1,0:T(8,128)(2,1)S(1)}, u32[]{:S(2)}, u32[]{:S(2)}) %collective-permute-start.7) | collective-permute-done | bytes 811040 | tf_op jit(solution)/shard_map/ppermute | solution.py:148
  30.4 0.6 collective-permute-start.8
  31.0 2.1 %near.1.refs_6_ = f32[16,512]{1,0:T(8,128)S(1)} custom-call(bf16[528,768]{1,0:T(8,128)(2,1)S(1)} %pack.1.refs_0_.refs_3_.refs_1_.refs_2_, bf16[528,768]{1,0:T(8,128)(2,1)S(1)} %collective-permute-done.1.refs_1_, bf16[528,768]{1,0:T(8,128)(2,1)S(1)} %collective-permute-done.5.refs_2_.refs_4_.refs_3_, ...), custom_call_target="tpu_custom_call" | custom-call | tf_op jit(solution)/shard_map/near/pallas_call | solution.py:127
  33.2 3.2 %column.1.refs_7_ = f32[16,512]{1,0:T(8,128)S(1)} custom-call(bf16[528,768]{1,0:T(8,128)(2,1)S(1)} %collective-permute-done.2.refs_0_.refs_2_, bf16[272,768]{1,0:T(8,128)(2,1)S(1)} %collective-permute-done.3.refs_1_.refs_3_, bf16[256,768]{1,0:T(8,128)(2,1)S(1)} %collective-permute-done.4.refs_2_.refs_4_, ...), custom_call_target="tpu_custom_call" | custom-call | tf_op jit(solution)/shard_map/column/pallas_call | solution.py:127
  36.4 1.8 %collective-permute-done.8.refs_6_.refs_5_ = bf16[208,768]{1,0:T(8,128)(2,1)S(1)} collective-permute-done((bf16[208,768]{1,0:T(8,128)(2,1)S(1)}, bf16[208,768]{1,0:T(8,128)(2,1)S(1)}, u32[]{:S(2)}, u32[]{:S(2)}) %collective-permute-start.8) | collective-permute-done | bytes 319520 | tf_op jit(solution)/shard_map/ppermute | solution.py:148
  38.1 1.7 %collective-permute-done.6.refs_5_.refs_4_ = bf16[320,768]{1,0:T(8,128)(2,1)S(1)} collective-permute-done((bf16[320,768]{1,0:T(8,128)(2,1)S(1)}, bf16[320,768]{1,0:T(8,128)(2,1)S(1)}, u32[]{:S(2)}, u32[]{:S(2)}) %collective-permute-start.6) | collective-permute-done | bytes 491552 | tf_op jit(solution)/shard_map/ppermute | solution.py:148
  39.8 2.3 %far.1.refs_6_ = f32[16,512]{1,0:T(8,128)S(1)} custom-call(bf16[528,768]{1,0:T(8,128)(2,1)S(1)} %pack.1.refs_0_.refs_3_.refs_1_.refs_2_, bf16[528,768]{1,0:T(8,128)(2,1)S(1)} %collective-permute-done.1.refs_1_, bf16[528,768]{1,0:T(8,128)(2,1)S(1)} %collective-permute-done.2.refs_0_.refs_2_, bf16[272,768]{1,0:T(8,128)(2,1)S(1)} %collective-permute-done.3.refs_1_.refs_3_, ...), custom_call_target="tpu_custom_call" | custom-call | tf_op jit(solution)/shard_map/far/pallas_call | solution.py:127
  42.1 2.4 %collective-permute-done.refs_0_ = bf16[528,768]{1,0:T(8,128)(2,1)S(1)} collective-permute-done((bf16[528,768]{1,0:T(8,128)(2,1)S(1)}, bf16[528,768]{1,0:T(8,128)(2,1)S(1)}, u32[]{:S(2)}, u32[]{:S(2)}) %collective-permute-start) | collective-permute-done | bytes 811040 | tf_op jit(solution)/shard_map/ppermute | solution.py:158
  44.6 0.6 collective-permute-start.9
  45.2 1.5 %collective-permute-start.11 = (f32[2,512]{1,0:T(2,128)S(1)}, f32[2,512]{1,0:T(2,128)S(1)}, u32[]{:S(2)}, u32[]{:S(2)}) collective-permute-start(f32[2,512]{1,0:T(2,128)S(1)} %slice.62), channel_id=1, source_target_pairs={{0,2},{1,3},{2,4},{3,5},{4,6},{5,7},{6,0},{7,1},{8,10},{9,11},{10,... | collective-permute-start | bytes 12296 | tf_op jit(solution)/shard_map/ppermute | solution.py:158
  46.7 2.1 %last.1.refs_6_ = f32[16,512]{1,0:T(8,128)S(1)} custom-call(bf16[528,768]{1,0:T(8,128)(2,1)S(1)} %collective-permute-done.refs_0_, bf16[528,768]{1,0:T(8,128)(2,1)S(1)} %pack.1.refs_0_.refs_3_.refs_1_.refs_2_, bf16[528,768]{1,0:T(8,128)(2,1)S(1)} %collective-permute-done.5.refs_2_.refs_4_.refs_3_, ...), custom_call_target="tpu_custom_call" | custom-call | tf_op jit(solution)/shard_map/last/pallas_call | solution.py:127
  48.8 1.2 %end.1.refs_7_ = f32[16,512]{1,0:T(8,128)S(1)} custom-call(bf16[272,768]{1,0:T(8,128)(2,1)S(1)} %collective-permute-done.10.refs_0_.refs_1_, bf16[528,768]{1,0:T(8,128)(2,1)S(1)} %pack.1.refs_0_.refs_3_.refs_1_.refs_2_, bf16[528,768]{1,0:T(8,128)(2,1)S(1)} %collective-permute-done.5.refs_2_.refs_4_.refs_3_, ...), custom_call_target="tpu_custom_call" | custom-call | tf_op jit(solution)/shard_map/end/pallas_call | solution.py:127
  50.1 0.5 collective-permute-done.11
  50.6 1.2 %top.1 = f32[16,512]{1,0:T(8,128)S(1)} custom-call(bf16[256,768]{1,0:T(8,128)(2,1)S(1)} %collective-permute-done.9.refs_0_, bf16[272,768]{1,0:T(8,128)(2,1)S(1)} %collective-permute-done.10.refs_0_.refs_1_, bf16[528,768]{1,0:T(8,128)(2,1)S(1)} %pack.1.refs_0_.refs_3_.refs_1_.refs_2_, bf16[528,768]{1,0:T(8,128)(2,1)S(1)} %collective-permute-done.5.refs_2_.refs_4_.refs_3_, ...), custom_call_target="tpu_custom_call" | custom-call | tf_op jit(solution)/shard_map/top/pallas_call | solution.py:127
  51.8 1.6 %collective-permute-start.12 = (f32[2,512]{1,0:T(2,128)S(1)}, f32[2,512]{1,0:T(2,128)S(1)}, u32[]{:S(2)}, u32[]{:S(2)}) collective-permute-start(f32[2,512]{1,0:T(2,128)S(1)} %slice.64), channel_id=1, source_target_pairs={{0,4},{1,5},{2,6},{3,7},{4,0},{5,1},{6,2},{7,3},{8,12},{9,13},{10,... | collective-permute-start | bytes 12296 | tf_op jit(solution)/shard_map/ppermute | solution.py:158
  53.5 0.6 collective-permute-start.14
  54.1 1.5 %collective-permute-start.15 = (f32[512]{0:T(512)S(1)}, f32[512]{0:T(512)S(1)}, u32[]{:S(2)}, u32[]{:S(2)}) collective-permute-start(f32[512]{0:T(512)S(1)} %bitcast.14), channel_id=1, source_target_pairs={{0,16},{1,17},{2,18},{3,19},{4,20},{5,21},{6,22},{7,23},{8,24},{9,... | collective-permute-start | bytes 6152 | tf_op jit(solution)/shard_map/ppermute | solution.py:148
  55.6 1.4 %collective-permute-start.16 = (f32[512]{0:T(512)S(1)}, f32[512]{0:T(512)S(1)}, u32[]{:S(2)}, u32[]{:S(2)}) collective-permute-start(f32[512]{0:T(512)S(1)} %bitcast.13), channel_id=1, source_target_pairs={{0,24},{1,25},{2,26},{3,27},{4,28},{5,29},{6,30},{7,31},{8,16},{9,... | collective-permute-start | bytes 6152 | tf_op jit(solution)/shard_map/ppermute | solution.py:148
  57.7 2.4 %collective-permute-done.16 = f32[512]{0:T(512)S(1)} collective-permute-done((f32[512]{0:T(512)S(1)}, f32[512]{0:T(512)S(1)}, u32[]{:S(2)}, u32[]{:S(2)}) %collective-permute-start.16) | collective-permute-done | bytes 2080 | tf_op jit(solution)/shard_map/ppermute | solution.py:148
  60.1 0.6 maximum_maximum_fusion
  (28 shorter events, 1.7 us)
Async XLA Ops:
  0.0 0.7 %copy-start.1 = (s32[512,1]{0,1:T(1,128)S(1)}, s32[512,1]{0,1:T(1,128)}, u32[]{:S(2)}) copy-start(s32[512,1]{0,1:T(1,128)} %param.4) | copy-start | bytes 6148
  1.4 1.1 %copy-start = (bf16[512,768]{1,0:T(8,128)(2,1)S(1)}, bf16[512,768]{1,0:T(8,128)(2,1)}, u32[]{:S(2)}) copy-start(bf16[512,768]{1,0:T(8,128)(2,1)} %values_ref.1) | copy-start | bytes 2359300
  2.8 9.6 %collective-permute-start.1 = (bf16[528,768]{1,0:T(8,128)(2,1)S(1)}, bf16[528,768]{1,0:T(8,128)(2,1)S(1)}, u32[]{:S(2)}, u32[]{:S(2)}) collective-permute-start(bf16[528,768]{1,0:T(8,128)(2,1)S(1)} %pack.1.refs_0_.refs_3_.refs_1_.refs_2_), channel_id=1, source_target_pairs={{0,1},{1,0},{2,3},{3,2},{4,5},{5,4},{6,7},{7,6},{8,9},{9,8},{10,11... | collective-permute-start | bytes 2433032 | tf_op jit(solution)/shard_map/ppermute | solution.py:152
  3.3 21.2 %collective-permute-start.5 = (bf16[528,768]{1,0:T(8,128)(2,1)S(1)}, bf16[528,768]{1,0:T(8,128)(2,1)S(1)}, u32[]{:S(2)}, u32[]{:S(2)}) collective-permute-start(bf16[528,768]{1,0:T(8,128)(2,1)S(1)} %pack.1.refs_0_.refs_3_.refs_1_.refs_2_), channel_id=1, source_target_pairs={{0,8},{1,9},{2,10},{3,11},{4,12},{5,13},{6,14},{7,15},{8,0},{9,1},... | collective-permute-start | bytes 2433032 | tf_op jit(solution)/shard_map/ppermute | solution.py:148
  5.8 22.0 %collective-permute-start.2 = (bf16[528,768]{1,0:T(8,128)(2,1)S(1)}, bf16[528,768]{1,0:T(8,128)(2,1)S(1)}, u32[]{:S(2)}, u32[]{:S(2)}) collective-permute-start(bf16[528,768]{1,0:T(8,128)(2,1)S(1)} %pack.1.refs_0_.refs_3_.refs_1_.refs_2_), channel_id=1, source_target_pairs={{0,6},{1,7},{2,0},{3,1},{4,2},{5,3},{6,4},{7,5},{8,14},{9,15},{10,... | collective-permute-start | bytes 2433032 | tf_op jit(solution)/shard_map/ppermute | solution.py:158
  9.4 21.0 %collective-permute-start.7 = (bf16[528,768]{1,0:T(8,128)(2,1)S(1)}, bf16[528,768]{1,0:T(8,128)(2,1)S(1)}, u32[]{:S(2)}, u32[]{:S(2)}) collective-permute-start(bf16[528,768]{1,0:T(8,128)(2,1)S(1)} %pack.1.refs_0_.refs_3_.refs_1_.refs_2_), channel_id=1, source_target_pairs={{0,16},{1,17},{2,18},{3,19},{4,20},{5,21},{6,22},{7,23},{8,24},{9,... | collective-permute-start | bytes 2433032 | tf_op jit(solution)/shard_map/ppermute | solution.py:148
  11.0 33.5 %collective-permute-start = (bf16[528,768]{1,0:T(8,128)(2,1)S(1)}, bf16[528,768]{1,0:T(8,128)(2,1)S(1)}, u32[]{:S(2)}, u32[]{:S(2)}) collective-permute-start(bf16[528,768]{1,0:T(8,128)(2,1)S(1)} %pack.1.refs_0_.refs_3_.refs_1_.refs_2_), channel_id=1, source_target_pairs={{0,4},{1,5},{6,2},{7,3},{8,12},{9,13},{14,10},{15,11},{16,20},{17,... | collective-permute-start | bytes 2433032 | tf_op jit(solution)/shard_map/ppermute | solution.py:158
  24.5 15.3 %collective-permute-start.6 = (bf16[320,768]{1,0:T(8,128)(2,1)S(1)}, bf16[320,768]{1,0:T(8,128)(2,1)S(1)}, u32[]{:S(2)}, u32[]{:S(2)}) collective-permute-start(bf16[320,768]{1,0:T(8,128)(2,1)S(1)} %slice.47), channel_id=1, source_target_pairs={{0,16},{1,17},{2,18},{3,19},{4,20},{5,21},{6,22},{7,23},{8,24},{9,... | collective-permute-start | bytes 1474568 | tf_op jit(solution)/shard_map/ppermute | solution.py:148
  27.9 5.2 %collective-permute-start.3 = (bf16[272,768]{1,0:T(8,128)(2,1)S(1)}, bf16[272,768]{1,0:T(8,128)(2,1)S(1)}, u32[]{:S(2)}, u32[]{:S(2)}) collective-permute-start(bf16[272,768]{1,0:T(8,128)(2,1)S(1)} %slice.60), channel_id=1, source_target_pairs={{0,1},{1,0},{2,3},{3,2},{4,5},{5,4},{6,7},{7,6},{8,9},{9,8},{10,11... | collective-permute-start | bytes 1253384 | tf_op jit(solution)/shard_map/ppermute | solution.py:152
  28.0 5.1 %collective-permute-start.4 = (bf16[256,768]{1,0:T(8,128)(2,1)S(1)}, bf16[256,768]{1,0:T(8,128)(2,1)S(1)}, u32[]{:S(2)}, u32[]{:S(2)}) collective-permute-start(bf16[256,768]{1,0:T(8,128)(2,1)S(1)} %slice.61), channel_id=1, source_target_pairs={{0,1},{1,0},{2,3},{3,2},{4,5},{5,4},{6,7},{7,6},{8,9},{9,8},{10,11... | collective-permute-start | bytes 1179656 | tf_op jit(solution)/shard_map/ppermute | solution.py:152
  30.4 7.7 %collective-permute-start.8 = (bf16[208,768]{1,0:T(8,128)(2,1)S(1)}, bf16[208,768]{1,0:T(8,128)(2,1)S(1)}, u32[]{:S(2)}, u32[]{:S(2)}) collective-permute-start(bf16[208,768]{1,0:T(8,128)(2,1)S(1)} %slice.48), channel_id=1, source_target_pairs={{0,8},{1,9},{2,10},{3,11},{4,12},{5,13},{6,14},{7,15},{8,0},{9,1},... | collective-permute-start | bytes 958472 | tf_op jit(solution)/shard_map/ppermute | solution.py:148
  44.5 4.3 %collective-permute-start.10 = (bf16[272,768]{1,0:T(8,128)(2,1)S(1)}, bf16[272,768]{1,0:T(8,128)(2,1)S(1)}, u32[]{:S(2)}, u32[]{:S(2)}) collective-permute-start(bf16[272,768]{1,0:T(8,128)(2,1)S(1)} %slice.50), channel_id=1, source_target_pairs={{0,1},{1,0},{2,3},{3,2},{4,5},{5,4},{6,7},{7,6},{8,9},{9,8},{10,11... | collective-permute-start | bytes 1253384 | tf_op jit(solution)/shard_map/ppermute | solution.py:152
  44.6 6.0 %collective-permute-start.9 = (bf16[256,768]{1,0:T(8,128)(2,1)S(1)}, bf16[256,768]{1,0:T(8,128)(2,1)S(1)}, u32[]{:S(2)}, u32[]{:S(2)}) collective-permute-start(bf16[256,768]{1,0:T(8,128)(2,1)S(1)} %slice.49), channel_id=1, source_target_pairs={{0,1},{1,0},{2,3},{3,2},{4,5},{5,4},{6,7},{7,6},{8,9},{9,8},{10,11... | collective-permute-start | bytes 1179656 | tf_op jit(solution)/shard_map/ppermute | solution.py:152
  45.2 5.4 %collective-permute-start.11 = (f32[2,512]{1,0:T(2,128)S(1)}, f32[2,512]{1,0:T(2,128)S(1)}, u32[]{:S(2)}, u32[]{:S(2)}) collective-permute-start(f32[2,512]{1,0:T(2,128)S(1)} %slice.62), channel_id=1, source_target_pairs={{0,2},{1,3},{2,4},{3,5},{4,6},{5,7},{6,0},{7,1},{8,10},{9,11},{10,... | collective-permute-start | bytes 12296 | tf_op jit(solution)/shard_map/ppermute | solution.py:158
  51.8 5.2 %collective-permute-start.12 = (f32[2,512]{1,0:T(2,128)S(1)}, f32[2,512]{1,0:T(2,128)S(1)}, u32[]{:S(2)}, u32[]{:S(2)}) collective-permute-start(f32[2,512]{1,0:T(2,128)S(1)} %slice.64), channel_id=1, source_target_pairs={{0,4},{1,5},{2,6},{3,7},{4,0},{5,1},{6,2},{7,3},{8,12},{9,13},{10,... | collective-permute-start | bytes 12296 | tf_op jit(solution)/shard_map/ppermute | solution.py:158
  53.5 3.7 %collective-permute-start.14 = (f32[512]{0:T(512)S(1)}, f32[512]{0:T(512)S(1)}, u32[]{:S(2)}, u32[]{:S(2)}) collective-permute-start(f32[512]{0:T(512)S(1)} %bitcast.15), channel_id=1, source_target_pairs={{0,8},{1,9},{2,10},{3,11},{4,12},{5,13},{6,14},{7,15},{8,0},{9,1},... | collective-permute-start | bytes 6152 | tf_op jit(solution)/shard_map/ppermute | solution.py:148
  54.1 3.6 %collective-permute-start.15 = (f32[512]{0:T(512)S(1)}, f32[512]{0:T(512)S(1)}, u32[]{:S(2)}, u32[]{:S(2)}) collective-permute-start(f32[512]{0:T(512)S(1)} %bitcast.14), channel_id=1, source_target_pairs={{0,16},{1,17},{2,18},{3,19},{4,20},{5,21},{6,22},{7,23},{8,24},{9,... | collective-permute-start | bytes 6152 | tf_op jit(solution)/shard_map/ppermute | solution.py:148
  55.6 4.5 %collective-permute-start.16 = (f32[512]{0:T(512)S(1)}, f32[512]{0:T(512)S(1)}, u32[]{:S(2)}, u32[]{:S(2)}) collective-permute-start(f32[512]{0:T(512)S(1)} %bitcast.13), channel_id=1, source_target_pairs={{0,24},{1,25},{2,26},{3,27},{4,28},{5,29},{6,30},{7,31},{8,16},{9,... | collective-permute-start | bytes 6152 | tf_op jit(solution)/shard_map/ppermute | solution.py:148
  57.1 3.0 %collective-permute-start.13 = (f32[512]{0:T(512)S(1)}, f32[512]{0:T(512)S(1)}, u32[]{:S(2)}, u32[]{:S(2)}) collective-permute-start(f32[512]{0:T(512)S(1)} %bitcast.12), channel_id=1, source_target_pairs={{0,1},{1,0},{2,3},{3,2},{4,5},{5,4},{6,7},{7,6},{8,9},{9,8},{10,11... | collective-permute-start | bytes 6152 | tf_op jit(solution)/shard_map/ppermute | solution.py:152

commit v3 on v2

--- a/solution.py
+++ b/solution.py
@@ -10,6 +10,7 @@
 F32 = jnp.float32
 BF16 = jnp.bfloat16
 KEYS = 16
+PARTS = 4
 VMEM_LIMIT = 32 * 1024 * 1024
 
 
@@ -31,28 +32,47 @@
     return jnp.transpose(jnp.broadcast_to(row, (8, row.shape[1])))[:length, 0:1]
 
 
-def pack_kernel(values_ref, marks_ref, full_ref):
+def pack_kernel(values_ref, cluster_ref, order_ref, full_ref, values, cluster, order, sems):
     rows, width = values_ref.shape
-    values = values_ref[...].astype(F32)
-    unit = values * lax.rsqrt(jnp.sum(values * values, axis=1, keepdims=True) + 1e-06)
-    full_ref[0:rows, :] = unit.astype(BF16)
-    order, cluster = marks_ref[0:1, :], marks_ref[1:2, :]
-    kept = [order & 127, (order >> 7) & 127, order >> 14, cluster + 1]
-    kept += [jnp.zeros_like(order)] * (KEYS - len(kept))
+    step = rows // PARTS
+    spans = [pl.ds(i * step, step) for i in range(PARTS)]
+    copies = [pltpu.make_async_copy(values_ref.at[span], values.at[span], sems.at[i]) for i, span in enumerate(spans)]
+    copies.append(pltpu.make_async_copy(cluster_ref, cluster, sems.at[PARTS]))
+    copies.append(pltpu.make_async_copy(order_ref, order, sems.at[PARTS + 1]))
+    for copy in copies:
+        copy.start()
+    for i in range(PARTS):
+        copies[i].wait()
+        part = values[i * step : (i + 1) * step, :].astype(F32)
+        unit = part * lax.rsqrt(jnp.sum(part * part, axis=1, keepdims=True) + 1e-06)
+        full_ref[i * step : (i + 1) * step, :] = unit.astype(BF16)
+    copies[PARTS].wait()
+    copies[PARTS + 1].wait()
+    orders = order[...]
+    kept = [orders & 127, (orders >> 7) & 127, orders >> 14, cluster[...] + 1]
+    kept += [jnp.zeros_like(orders)] * (KEYS - len(kept))
     keys = jnp.concatenate(kept, axis=0).astype(F32).astype(BF16)
     if width > rows:
         keys = jnp.concatenate([keys, jnp.zeros((KEYS, width - rows), BF16)], axis=1)
     full_ref[rows : rows + KEYS, :] = keys
 
 
-def pack(values, marks):
+def pack(values, cluster, order):
     rows, width = values.shape
+    held = [pltpu.with_memory_space_constraint(x, pltpu.HBM) for x in (values, cluster, order)]
     return pl.pallas_call(
         pack_kernel,
         out_shape=jax.ShapeDtypeStruct((rows + KEYS, width), BF16),
+        in_specs=[pl.BlockSpec(memory_space=pltpu.HBM)] * 3,
+        scratch_shapes=[
+            pltpu.VMEM(values.shape, BF16),
+            pltpu.VMEM(cluster.shape, jnp.int32),
+            pltpu.VMEM(order.shape, jnp.int32),
+            pltpu.SemaphoreType.DMA((PARTS + 2,)),
+        ],
         compiler_params=pltpu.CompilerParams(vmem_limit_bytes=VMEM_LIMIT),
         name="pack",
-    )(values, marks)
+    )(*held)
 
 
 def row_range(arrays, parts, low, count):
@@ -159,9 +179,9 @@
 
     rounds = plane_rounds(planes)
     n_rounds = len(rounds)
-    half, near_cut = rows // 2, 5 * rows // 8
+    half, near_cut, cut = rows // 2, rows // 2, 3 * rows // 8
     last = n_bulk - 1
-    full = pack(embeddings, jnp.stack([row_order, cluster_ids.reshape(rows)]))
+    full = pack(embeddings, cluster_ids.reshape(1, rows), row_order.reshape(1, rows))
 
     own_line, t_line = 0, 1
     z_line, tz_line = lambda k: 2 + 2 * k, lambda k: 3 + 2 * k
@@ -186,19 +206,19 @@
     same = [whole(full, own_line, False), whole(twin, t_line, False)]
     blocks = [block(full, p_line(0))]
     best = fold(best, same, blocks, "own")
-    bulk = [full] + [after(x, best) for x in bulk]
+    bulk = [full] + bulk
     d_top = bulk_move(bulk[1][:near_cut], last ^ 1)
     d_end = bulk_move(bulk[last ^ 1][near_cut:], 1)
     k = n_rounds - 1
-    z_twin = [(core_move(x[:half]), core_move(x[half:])) for x in z[:k]]
+    z_twin = [(core_move(x[:cut]), core_move(x[cut:])) for x in z[:k]]
     near = [block(bulk[j], p_line(j)) for j in range(1, last)]
     far = [([(d_top, 0, near_cut), (d_end, 0, rows - near_cut)], d_end, rows - near_cut, p_line(last))]
     most = []
     for r in range(k):
         top, end = z_twin[r]
         most.append(whole(z[r], z_line(r), True))
-        most.append((end, 0, half, end, half, half, tz_line(r), True))
-        most.append((top, 0, half, end, half, 0, tz_line(r), True))
+        most.append((end, 0, rows - cut, end, rows - cut, cut, tz_line(r), True))
+        most.append((top, 0, cut, end, rows - cut, 0, tz_line(r), True))
     best = fold(best, same, near, "near")
     best = fold(best, most, blocks + near, "column")
     best = fold(best, same + most, far, "far")
@@ -206,17 +226,16 @@
     parts = [go_home(best[z_line(r) : tz_line(r) + 1], r) for r in range(k)]
     blocks += near + far
     z_last = after(z[k], best)
-    z_top, z_end = core_move(z_last[:half]), core_move(z_last[half:])
+    z_last_twin = core_move(z_last)
     best = fold(best, [whole(z_last, z_line(k), True)], blocks, "last")
-    best = fold(best, [(z_end, 0, half, z_end, half, half, tz_line(k), True)], blocks, "end")
-    parts = [after(x, best) for x in parts]
-    best = fold(after(best, *parts), [(z_top, 0, half, z_end, half, 0, tz_line(k), True)], blocks, "top")
+    best = fold(best, [whole(z_last_twin, tz_line(k), True)], blocks, "rest")
 
     parts.append(go_home(best[z_line(k) : tz_line(k) + 1], k))
     both = functools.reduce(jnp.maximum, parts, best[own_line : t_line + 1])
     mine = best[p_line(0)]
-    for j in range(1, n_bulk):
+    for j in range(1, last):
         mine = jnp.maximum(mine, bulk_move(best[p_line(j)], j))
+    mine = jnp.maximum(mine, bulk_move(best, last)[p_line(last)])
     return jnp.maximum(jnp.maximum(both[0], core_move(both[1])), mine)
 
 

time: 60.9 us -> 56.7 us (0.931)
  waiting for transfers between devices: 23.4 us -> 19.8 us
  local copies, waits for them, and re-layouts: 2 us -> 0.14 us
  Pallas kernels: 13.8 us -> 15.1 us
  starting transfers between devices: 20 us -> 20.7 us
  other arithmetic: 1.28 us -> 0.59 us
    ppermute x7, waiting for transfers between devices: 19 us -> 4.91 us  [bulk_move(): return lax.ppermute(x, axes, pairs)]
    ppermute x4, waiting for transfers between devices: 4.39 us -> 14.9 us  [plane_move(): return lax.ppermute(x, axes, pairs)]
    ppermute x4, starting transfers between devices: 8.1 us -> 10.9 us  [plane_move(): return lax.ppermute(x, axes, pairs)]
    unnamed x4 -> x0, local copies, waits for them, and re-layouts: 1.81 us -> none
    ppermute x6 -> x5, starting transfers between devices: 1.84 us -> 0.22 us  [core_move(): return lax.ppermute(x, axes, pairs)]
    pallas_call x1, Pallas kernels: 0.25 us -> 1.5 us  [pack(): pl.pallas_call(pack_kernel, out_shape=jax.ShapeDtypeStruct((rows + KEYS,...]
    another operation x1 -> x0, other arithmetic: 0.69 us -> none  [on_device(): full = pack(embeddings, jnp.stack([row_order, cluster_ids.reshape(rows)]))]
    pallas_call x7 -> x6, Pallas kernels: 13.5 us -> 13.6 us  [fold(): pl.pallas_call(functools.partial(pair_kernel, (len(arrays), *plan)), out_...]
  transfers between devices with their start and end apart: 17 -> 16, of which waited for: 9 -> 7; matrix products, arithmetic and copies ran while one was open for 0% -> 0% of each run, Pallas kernels for 20% -> 24%
where the time goes in v3:
time: 56.7 us; the launch traced here: 56.5 us
  starting transfers between devices  20.7 us (37%)
  waiting for transfers between devices  19.8 us (35%)
  Pallas kernels  15.1 us (27%)
  other arithmetic  0.59 us (1%)
    ppermute x4, waiting for transfers between devices, plane_move(): return lax.ppermute(x, axes, pairs)  14.9 us
    pallas_call x6, Pallas kernels, fold(): pl.pallas_call(functools.partial(pair_kernel, (len(arrays), *plan)), out_...  13.6 us
    ppermute x4, starting transfers between devices, plane_move(): return lax.ppermute(x, axes, pairs)  10.9 us
    ppermute x7, starting transfers between devices, bulk_move(): return lax.ppermute(x, axes, pairs)  9.64 us
    ppermute x7, waiting for transfers between devices, bulk_move(): return lax.ppermute(x, axes, pairs)  4.91 us
    pallas_call x1, Pallas kernels, pack(): pl.pallas_call(pack_kernel, out_shape=jax.ShapeDtypeStruct((rows + KEYS,...  1.5 us
  transfers between devices with their start and end apart: 16, of which 7 were waited for; matrix products, arithmetic and copies ran while one was open for 0% of the time, Pallas kernels for 24%

profile of v3, /device:TPU:0, one launch (start us, length us, event | category | flops | bytes accessed | tf_op | source)
XLA Modules:
  0.0 56.5 jit_solution(4897238633171611442)
XLA Ops:
  0.0 1.5 %pack.1.refs_0_.refs_3_.refs_1_ = bf16[528,768]{1,0:T(8,128)(2,1)S(1)} custom-call(bf16[512,768]{1,0:T(8,128)(2,1)} %values_ref.1, s32[1,512]{1,0:T(1,128)} %bitcast.11, s32[1,512]{1,0:T(1,128)} %bitcast.12), custom_call_target="tpu_custom_call" | custom-call | tf_op jit(solution)/shard_map/pack/pallas_call | solution.py:63
  1.5 5.1 %collective-permute-start.2 = (bf16[528,768]{1,0:T(8,128)(2,1)S(1)}, bf16[528,768]{1,0:T(8,128)(2,1)S(1)}, u32[]{:S(2)}, u32[]{:S(2)}) collective-permute-start(bf16[528,768]{1,0:T(8,128)(2,1)S(1)} %pack.1.refs_0_.refs_3_.refs_1_), channel_id=1, source_target_pairs={{0,6},{1,7},{2,0},{3,1},{4,2},{5,3},{6,4},{7,5},{8,14},{9,15},{10,... | collective-permute-start | bytes 2433032 | tf_op jit(solution)/shard_map/ppermute | solution.py:178
  6.6 1.5 %collective-permute-start.7 = (bf16[528,768]{1,0:T(8,128)(2,1)S(1)}, bf16[528,768]{1,0:T(8,128)(2,1)S(1)}, u32[]{:S(2)}, u32[]{:S(2)}) collective-permute-start(bf16[528,768]{1,0:T(8,128)(2,1)S(1)} %pack.1.refs_0_.refs_3_.refs_1_), channel_id=1, source_target_pairs={{0,16},{1,17},{2,18},{3,19},{4,20},{5,21},{6,22},{7,23},{8,24},{9,... | collective-permute-start | bytes 2433032 | tf_op jit(solution)/shard_map/ppermute | solution.py:168
  8.1 1.5 %collective-permute-start.5 = (bf16[528,768]{1,0:T(8,128)(2,1)S(1)}, bf16[528,768]{1,0:T(8,128)(2,1)S(1)}, u32[]{:S(2)}, u32[]{:S(2)}) collective-permute-start(bf16[528,768]{1,0:T(8,128)(2,1)S(1)} %pack.1.refs_0_.refs_3_.refs_1_), channel_id=1, source_target_pairs={{0,8},{1,9},{2,10},{3,11},{4,12},{5,13},{6,14},{7,15},{8,0},{9,1},... | collective-permute-start | bytes 2433032 | tf_op jit(solution)/shard_map/ppermute | solution.py:168
  9.6 1.4 %collective-permute-start = (bf16[528,768]{1,0:T(8,128)(2,1)S(1)}, bf16[528,768]{1,0:T(8,128)(2,1)S(1)}, u32[]{:S(2)}, u32[]{:S(2)}) collective-permute-start(bf16[528,768]{1,0:T(8,128)(2,1)S(1)} %pack.1.refs_0_.refs_3_.refs_1_), channel_id=1, source_target_pairs={{0,4},{1,5},{6,2},{7,3},{8,12},{9,13},{14,10},{15,11},{16,20},{17,... | collective-permute-start | bytes 2433032 | tf_op jit(solution)/shard_map/ppermute | solution.py:178
  11.0 14.1 %collective-permute-done.2.refs_0_.refs_2_ = bf16[528,768]{1,0:T(8,128)(2,1)S(1)} collective-permute-done((bf16[528,768]{1,0:T(8,128)(2,1)S(1)}, bf16[528,768]{1,0:T(8,128)(2,1)S(1)}, u32[]{:S(2)}, u32[]{:S(2)}) %collective-permute-start.2) | collective-permute-done | bytes 811040 | tf_op jit(solution)/shard_map/ppermute | solution.py:178
  25.1 0.1 collective-permute-start.3
  25.2 0.9 %collective-permute-done.7.refs_3_.refs_5_ = bf16[528,768]{1,0:T(8,128)(2,1)S(1)} collective-permute-done((bf16[528,768]{1,0:T(8,128)(2,1)S(1)}, bf16[528,768]{1,0:T(8,128)(2,1)S(1)}, u32[]{:S(2)}, u32[]{:S(2)}) %collective-permute-start.7) | collective-permute-done | bytes 811040 | tf_op jit(solution)/shard_map/ppermute | solution.py:168
  26.2 1.6 %collective-permute-start.8 = (bf16[272,768]{1,0:T(8,128)(2,1)S(1)}, bf16[272,768]{1,0:T(8,128)(2,1)S(1)}, u32[]{:S(2)}, u32[]{:S(2)}) collective-permute-start(bf16[272,768]{1,0:T(8,128)(2,1)S(1)} %slice.55), channel_id=1, source_target_pairs={{0,8},{1,9},{2,10},{3,11},{4,12},{5,13},{6,14},{7,15},{8,0},{9,1},... | collective-permute-start | bytes 1253384 | tf_op jit(solution)/shard_map/ppermute | solution.py:168
  27.7 0.0 collective-permute-done.5.refs_2_.refs_4_
  27.8 1.6 %collective-permute-start.6 = (bf16[256,768]{1,0:T(8,128)(2,1)S(1)}, bf16[256,768]{1,0:T(8,128)(2,1)S(1)}, u32[]{:S(2)}, u32[]{:S(2)}) collective-permute-start(bf16[256,768]{1,0:T(8,128)(2,1)S(1)} %slice.54), channel_id=1, source_target_pairs={{0,16},{1,17},{2,18},{3,19},{4,20},{5,21},{6,22},{7,23},{8,24},{9,... | collective-permute-start | bytes 1179656 | tf_op jit(solution)/shard_map/ppermute | solution.py:168
  29.4 0.0 collective-permute-done.1.refs_1_
  29.4 0.1 collective-permute-start.4
  29.5 1.3 %own.1.refs_4_ = f32[16,512]{1,0:T(8,128)S(1)} custom-call(bf16[528,768]{1,0:T(8,128)(2,1)S(1)} %pack.1.refs_0_.refs_3_.refs_1_, bf16[528,768]{1,0:T(8,128)(2,1)S(1)} %collective-permute-done.1.refs_1_, f32[16,512]{1,0:T(8,128)S(1)} %broadcast_in_dim.3.refs_2_), custom_call_target="tpu_custom_call" | custom-call | tf_op jit(solution)/shard_map/own/pallas_call | solution.py:147
  30.8 2.1 %near.1.refs_6_ = f32[16,512]{1,0:T(8,128)S(1)} custom-call(bf16[528,768]{1,0:T(8,128)(2,1)S(1)} %pack.1.refs_0_.refs_3_.refs_1_, bf16[528,768]{1,0:T(8,128)(2,1)S(1)} %collective-permute-done.1.refs_1_, bf16[528,768]{1,0:T(8,128)(2,1)S(1)} %collective-permute-done.5.refs_2_.refs_4_, bf16[528,768]{1,0:T(8,128)(2,1)S(1)} %collective-permute-done.7.refs_3_.refs_5_, ...), custom_call_target="tpu_custom_call" | custom-call | tf_op jit(solution)/shard_map/near/pallas_call | solution.py:147
  32.9 0.0 collective-permute-done.4.refs_2_.refs_4_
  33.0 3.4 %column.1.refs_7_ = f32[16,512]{1,0:T(8,128)S(1)} custom-call(bf16[528,768]{1,0:T(8,128)(2,1)S(1)} %collective-permute-done.2.refs_0_.refs_2_, bf16[336,768]{1,0:T(8,128)(2,1)S(1)} %collective-permute-done.3.refs_1_.refs_3_, bf16[192,768]{1,0:T(8,128)(2,1)S(1)} %collective-permute-done.4.refs_2_.refs_4_, bf16[528,768]{1,0:T(8,128)(2,1)S(1)} %pack.1.refs_0_.refs_3_.refs_1_, ...), custom_call_target="tpu_custom_call" | custom-call | tf_op jit(solution)/shard_map/column/pallas_call | solution.py:147
  36.4 1.7 %collective-permute-done.6.refs_5_.refs_4_ = bf16[256,768]{1,0:T(8,128)(2,1)S(1)} collective-permute-done((bf16[256,768]{1,0:T(8,128)(2,1)S(1)}, bf16[256,768]{1,0:T(8,128)(2,1)S(1)}, u32[]{:S(2)}, u32[]{:S(2)}) %collective-permute-start.6) | collective-permute-done | bytes 393248 | tf_op jit(solution)/shard_map/ppermute | solution.py:168
  38.1 2.3 %far.1.refs_6_ = f32[16,512]{1,0:T(8,128)S(1)} custom-call(bf16[528,768]{1,0:T(8,128)(2,1)S(1)} %pack.1.refs_0_.refs_3_.refs_1_, bf16[528,768]{1,0:T(8,128)(2,1)S(1)} %collective-permute-done.1.refs_1_, bf16[528,768]{1,0:T(8,128)(2,1)S(1)} %collective-permute-done.2.refs_0_.refs_2_, bf16[336,768]{1,0:T(8,128)(2,1)S(1)} %collective-permute-done.3.refs_1_.refs_3_, ...), custom_call_target="tpu_custom_call" | custom-call | tf_op jit(solution)/shard_map/far/pallas_call | solution.py:147
  40.5 0.8 %collective-permute-done.refs_0_ = bf16[528,768]{1,0:T(8,128)(2,1)S(1)} collective-permute-done((bf16[528,768]{1,0:T(8,128)(2,1)S(1)}, bf16[528,768]{1,0:T(8,128)(2,1)S(1)}, u32[]{:S(2)}, u32[]{:S(2)}) %collective-permute-start) | collective-permute-done | bytes 811040 | tf_op jit(solution)/shard_map/ppermute | solution.py:178
  41.3 1.7 %collective-permute-start.10 = (f32[2,512]{1,0:T(2,128)S(1)}, f32[2,512]{1,0:T(2,128)S(1)}, u32[]{:S(2)}, u32[]{:S(2)}) collective-permute-start(f32[2,512]{1,0:T(2,128)S(1)} %slice.57), channel_id=1, source_target_pairs={{0,2},{1,3},{2,4},{3,5},{4,6},{5,7},{6,0},{7,1},{8,10},{9,11},{10,... | collective-permute-start | bytes 12296 | tf_op jit(solution)/shard_map/ppermute | solution.py:178
  43.0 2.2 %last.1.refs_6_ = f32[16,512]{1,0:T(8,128)S(1)} custom-call(bf16[528,768]{1,0:T(8,128)(2,1)S(1)} %collective-permute-done.refs_0_, bf16[528,768]{1,0:T(8,128)(2,1)S(1)} %pack.1.refs_0_.refs_3_.refs_1_, bf16[528,768]{1,0:T(8,128)(2,1)S(1)} %collective-permute-done.5.refs_2_.refs_4_, bf16[528,768]{1,0:T(8,128)(2,1)S(1)} %collective-permute-done.7.refs_3_.refs_5_, ...), custom_call_target="tpu_custom_call" | custom-call | tf_op jit(solution)/shard_map/last/pallas_call | solution.py:147
  45.2 2.2 %rest.1 = f32[16,512]{1,0:T(8,128)S(1)} custom-call(bf16[528,768]{1,0:T(8,128)(2,1)S(1)} %collective-permute-done.9.refs_0_, bf16[528,768]{1,0:T(8,128)(2,1)S(1)} %pack.1.refs_0_.refs_3_.refs_1_, bf16[528,768]{1,0:T(8,128)(2,1)S(1)} %collective-permute-done.5.refs_2_.refs_4_, bf16[528,768]{1,0:T(8,128)(2,1)S(1)} %collective-permute-done.7.refs_3_.refs_5_, ...), custom_call_target="tpu_custom_call" | custom-call | tf_op jit(solution)/shard_map/rest/pallas_call | solution.py:147
  47.4 2.7 %collective-permute-start.11 = (f32[2,512]{1,0:T(2,128)S(1)}, f32[2,512]{1,0:T(2,128)S(1)}, u32[]{:S(2)}, u32[]{:S(2)}) collective-permute-start(f32[2,512]{1,0:T(2,128)S(1)} %slice.58), channel_id=1, source_target_pairs={{0,4},{1,5},{2,6},{3,7},{4,0},{5,1},{6,2},{7,3},{8,12},{9,13},{10,... | collective-permute-start | bytes 12296 | tf_op jit(solution)/shard_map/ppermute | solution.py:178
  50.1 1.8 %collective-permute-start.15 = (f32[16,512]{1,0:T(8,128)S(1)}, f32[16,512]{1,0:T(8,128)S(1)}, u32[]{:S(2)}, u32[]{:S(2)}) collective-permute-start(f32[16,512]{1,0:T(8,128)S(1)} %rest.1), channel_id=1, source_target_pairs={{0,24},{1,25},{2,26},{3,27},{4,28},{5,29},{6,30},{7,31},{8,16},{9,... | collective-permute-start | bytes 98312 | tf_op jit(solution)/shard_map/ppermute | solution.py:168
  51.9 0.5 collective-permute-start.14
  52.4 1.2 %collective-permute-start.13 = (f32[512]{0:T(512)S(1)}, f32[512]{0:T(512)S(1)}, u32[]{:S(2)}, u32[]{:S(2)}) collective-permute-start(f32[512]{0:T(512)S(1)} %bitcast.13), channel_id=1, source_target_pairs={{0,8},{1,9},{2,10},{3,11},{4,12},{5,13},{6,14},{7,15},{8,0},{9,1},... | collective-permute-start | bytes 6152 | tf_op jit(solution)/shard_map/ppermute | solution.py:168
  53.6 0.1 collective-permute-start.12
  53.7 1.2 %collective-permute-done.15 = f32[16,512]{1,0:T(8,128)S(1)} collective-permute-done((f32[16,512]{1,0:T(8,128)S(1)}, f32[16,512]{1,0:T(8,128)S(1)}, u32[]{:S(2)}, u32[]{:S(2)}) %collective-permute-start.15) | collective-permute-done | bytes 32800 | tf_op jit(solution)/shard_map/ppermute | solution.py:168
  54.9 0.5 collective-permute-done.14
  55.4 0.5 collective-permute-done.13
  55.9 0.6 %maximum_maximum_fusion = f32[512]{0:T(512)} fusion(f32[512]{0:T(512)S(1)} %bitcast.8, f32[512]{0:T(512)S(1)} %collective-permute-done.14, f32[512]{0:T(512)S(1)} %bitcast.9, f32[512]{0:T(512)S(1)} %collective-permute-done.13, f32[512]{0:T(512)S(1)} %bitcast.10, f32[512]{0:T(512)S(1)} %collective-permute-done.12), kind=kLoop, calls=%fused_computation.2 | loop fusion | flops 2560 | bytes 14336 | tf_op jit(solution)/shard_map/max | solution.py:239
  (19 shorter events, 0.2 us)
Async XLA Ops:
  1.5 23.6 %collective-permute-start.2 = (bf16[528,768]{1,0:T(8,128)(2,1)S(1)}, bf16[528,768]{1,0:T(8,128)(2,1)S(1)}, u32[]{:S(2)}, u32[]{:S(2)}) collective-permute-start(bf16[528,768]{1,0:T(8,128)(2,1)S(1)} %pack.1.refs_0_.refs_3_.refs_1_), channel_id=1, source_target_pairs={{0,6},{1,7},{2,0},{3,1},{4,2},{5,3},{6,4},{7,5},{8,14},{9,15},{10,... | collective-permute-start | bytes 2433032 | tf_op jit(solution)/shard_map/ppermute | solution.py:178
  6.6 19.5 %collective-permute-start.7 = (bf16[528,768]{1,0:T(8,128)(2,1)S(1)}, bf16[528,768]{1,0:T(8,128)(2,1)S(1)}, u32[]{:S(2)}, u32[]{:S(2)}) collective-permute-start(bf16[528,768]{1,0:T(8,128)(2,1)S(1)} %pack.1.refs_0_.refs_3_.refs_1_), channel_id=1, source_target_pairs={{0,16},{1,17},{2,18},{3,19},{4,20},{5,21},{6,22},{7,23},{8,24},{9,... | collective-permute-start | bytes 2433032 | tf_op jit(solution)/shard_map/ppermute | solution.py:168
  8.1 19.6 %collective-permute-start.5 = (bf16[528,768]{1,0:T(8,128)(2,1)S(1)}, bf16[528,768]{1,0:T(8,128)(2,1)S(1)}, u32[]{:S(2)}, u32[]{:S(2)}) collective-permute-start(bf16[528,768]{1,0:T(8,128)(2,1)S(1)} %pack.1.refs_0_.refs_3_.refs_1_), channel_id=1, source_target_pairs={{0,8},{1,9},{2,10},{3,11},{4,12},{5,13},{6,14},{7,15},{8,0},{9,1},... | collective-permute-start | bytes 2433032 | tf_op jit(solution)/shard_map/ppermute | solution.py:168
  9.6 19.8 %collective-permute-start.1 = (bf16[528,768]{1,0:T(8,128)(2,1)S(1)}, bf16[528,768]{1,0:T(8,128)(2,1)S(1)}, u32[]{:S(2)}, u32[]{:S(2)}) collective-permute-start(bf16[528,768]{1,0:T(8,128)(2,1)S(1)} %pack.1.refs_0_.refs_3_.refs_1_), channel_id=1, source_target_pairs={{0,1},{1,0},{2,3},{3,2},{4,5},{5,4},{6,7},{7,6},{8,9},{9,8},{10,11... | collective-permute-start | bytes 2433032 | tf_op jit(solution)/shard_map/ppermute | solution.py:172
  9.6 31.7 %collective-permute-start = (bf16[528,768]{1,0:T(8,128)(2,1)S(1)}, bf16[528,768]{1,0:T(8,128)(2,1)S(1)}, u32[]{:S(2)}, u32[]{:S(2)}) collective-permute-start(bf16[528,768]{1,0:T(8,128)(2,1)S(1)} %pack.1.refs_0_.refs_3_.refs_1_), channel_id=1, source_target_pairs={{0,4},{1,5},{6,2},{7,3},{8,12},{9,13},{14,10},{15,11},{16,20},{17,... | collective-permute-start | bytes 2433032 | tf_op jit(solution)/shard_map/ppermute | solution.py:178
  25.1 7.8 %collective-permute-start.3 = (bf16[336,768]{1,0:T(8,128)(2,1)S(1)}, bf16[336,768]{1,0:T(8,128)(2,1)S(1)}, u32[]{:S(2)}, u32[]{:S(2)}) collective-permute-start(bf16[336,768]{1,0:T(8,128)(2,1)S(1)} %slice.52), channel_id=1, source_target_pairs={{0,1},{1,0},{2,3},{3,2},{4,5},{5,4},{6,7},{7,6},{8,9},{9,8},{10,11... | collective-permute-start | bytes 1548296 | tf_op jit(solution)/shard_map/ppermute | solution.py:172
  26.2 12.0 %collective-permute-start.8 = (bf16[272,768]{1,0:T(8,128)(2,1)S(1)}, bf16[272,768]{1,0:T(8,128)(2,1)S(1)}, u32[]{:S(2)}, u32[]{:S(2)}) collective-permute-start(bf16[272,768]{1,0:T(8,128)(2,1)S(1)} %slice.55), channel_id=1, source_target_pairs={{0,8},{1,9},{2,10},{3,11},{4,12},{5,13},{6,14},{7,15},{8,0},{9,1},... | collective-permute-start | bytes 1253384 | tf_op jit(solution)/shard_map/ppermute | solution.py:168
  27.8 10.4 %collective-permute-start.6 = (bf16[256,768]{1,0:T(8,128)(2,1)S(1)}, bf16[256,768]{1,0:T(8,128)(2,1)S(1)}, u32[]{:S(2)}, u32[]{:S(2)}) collective-permute-start(bf16[256,768]{1,0:T(8,128)(2,1)S(1)} %slice.54), channel_id=1, source_target_pairs={{0,16},{1,17},{2,18},{3,19},{4,20},{5,21},{6,22},{7,23},{8,24},{9,... | collective-permute-start | bytes 1179656 | tf_op jit(solution)/shard_map/ppermute | solution.py:168
  29.4 3.6 %collective-permute-start.4 = (bf16[192,768]{1,0:T(8,128)(2,1)S(1)}, bf16[192,768]{1,0:T(8,128)(2,1)S(1)}, u32[]{:S(2)}, u32[]{:S(2)}) collective-permute-start(bf16[192,768]{1,0:T(8,128)(2,1)S(1)} %slice.53), channel_id=1, source_target_pairs={{0,1},{1,0},{2,3},{3,2},{4,5},{5,4},{6,7},{7,6},{8,9},{9,8},{10,11... | collective-permute-start | bytes 884744 | tf_op jit(solution)/shard_map/ppermute | solution.py:172
  41.3 3.9 %collective-permute-start.9 = (bf16[528,768]{1,0:T(8,128)(2,1)S(1)}, bf16[528,768]{1,0:T(8,128)(2,1)S(1)}, u32[]{:S(2)}, u32[]{:S(2)}) collective-permute-start(bf16[528,768]{1,0:T(8,128)(2,1)S(1)} %collective-permute-done.refs_0_), channel_id=1, source_target_pairs={{0,1},{1,0},{2,3},{3,2},{4,5},{5,4},{6,7},{7,6},{8,9},{9,8},{10,11... | collective-permute-start | bytes 2433032 | tf_op jit(solution)/shard_map/ppermute | solution.py:172
  41.3 12.3 %collective-permute-start.10 = (f32[2,512]{1,0:T(2,128)S(1)}, f32[2,512]{1,0:T(2,128)S(1)}, u32[]{:S(2)}, u32[]{:S(2)}) collective-permute-start(f32[2,512]{1,0:T(2,128)S(1)} %slice.57), channel_id=1, source_target_pairs={{0,2},{1,3},{2,4},{3,5},{4,6},{5,7},{6,0},{7,1},{8,10},{9,11},{10,... | collective-permute-start | bytes 12296 | tf_op jit(solution)/shard_map/ppermute | solution.py:178
  47.4 6.2 %collective-permute-start.11 = (f32[2,512]{1,0:T(2,128)S(1)}, f32[2,512]{1,0:T(2,128)S(1)}, u32[]{:S(2)}, u32[]{:S(2)}) collective-permute-start(f32[2,512]{1,0:T(2,128)S(1)} %slice.58), channel_id=1, source_target_pairs={{0,4},{1,5},{2,6},{3,7},{4,0},{5,1},{6,2},{7,3},{8,12},{9,13},{10,... | collective-permute-start | bytes 12296 | tf_op jit(solution)/shard_map/ppermute | solution.py:178
  50.1 4.8 %collective-permute-start.15 = (f32[16,512]{1,0:T(8,128)S(1)}, f32[16,512]{1,0:T(8,128)S(1)}, u32[]{:S(2)}, u32[]{:S(2)}) collective-permute-start(f32[16,512]{1,0:T(8,128)S(1)} %rest.1), channel_id=1, source_target_pairs={{0,24},{1,25},{2,26},{3,27},{4,28},{5,29},{6,30},{7,31},{8,16},{9,... | collective-permute-start | bytes 98312 | tf_op jit(solution)/shard_map/ppermute | solution.py:168
  51.9 3.6 %collective-permute-start.14 = (f32[512]{0:T(512)S(1)}, f32[512]{0:T(512)S(1)}, u32[]{:S(2)}, u32[]{:S(2)}) collective-permute-start(f32[512]{0:T(512)S(1)} %bitcast.14), channel_id=1, source_target_pairs={{0,16},{1,17},{2,18},{3,19},{4,20},{5,21},{6,22},{7,23},{8,24},{9,... | collective-permute-start | bytes 6152 | tf_op jit(solution)/shard_map/ppermute | solution.py:168
  52.4 3.6 %collective-permute-start.13 = (f32[512]{0:T(512)S(1)}, f32[512]{0:T(512)S(1)}, u32[]{:S(2)}, u32[]{:S(2)}) collective-permute-start(f32[512]{0:T(512)S(1)} %bitcast.13), channel_id=1, source_target_pairs={{0,8},{1,9},{2,10},{3,11},{4,12},{5,13},{6,14},{7,15},{8,0},{9,1},... | collective-permute-start | bytes 6152 | tf_op jit(solution)/shard_map/ppermute | solution.py:168
  53.6 2.3 %collective-permute-start.12 = (f32[512]{0:T(512)S(1)}, f32[512]{0:T(512)S(1)}, u32[]{:S(2)}, u32[]{:S(2)}) collective-permute-start(f32[512]{0:T(512)S(1)} %bitcast.15), channel_id=1, source_target_pairs={{0,1},{1,0},{2,3},{3,2},{4,5},{5,4},{6,7},{7,6},{8,9},{9,8},{10,11... | collective-permute-start | bytes 6152 | tf_op jit(solution)/shard_map/ppermute | solution.py:172

commit v4 on v3

--- a/solution.py
+++ b/solution.py
@@ -10,7 +10,7 @@
 F32 = jnp.float32
 BF16 = jnp.bfloat16
 KEYS = 16
-PARTS = 4
+PARTS = 2
 VMEM_LIMIT = 32 * 1024 * 1024
 
 
@@ -219,7 +219,8 @@
         most.append(whole(z[r], z_line(r), True))
         most.append((end, 0, rows - cut, end, rows - cut, cut, tz_line(r), True))
         most.append((top, 0, cut, end, rows - cut, 0, tz_line(r), True))
-    best = fold(best, same, near, "near")
+    for j in range(len(near)):
+        best = fold(best, same, near[j : j + 1], "near")
     best = fold(best, most, blocks + near, "column")
     best = fold(best, same + most, far, "far")
 

time: 56.7 us -> 56.6 us (level)
    pallas_call x6 -> x7, Pallas kernels: 13.6 us -> 14.1 us  [fold(): pl.pallas_call(functools.partial(pair_kernel, (len(arrays), *plan)), out_...]
  transfers between devices with their start and end apart: 16 -> 16, of which waited for: 7 -> 7; matrix products, arithmetic and copies ran while one was open for 0% -> 0% of each run, Pallas kernels for 24% -> 25%
where the time goes in v4:
time: 56.6 us; the launch traced here: 56.4 us
  starting transfers between devices  20.7 us (37%)
  waiting for transfers between devices  19.4 us (34%)
  Pallas kernels  15.4 us (27%)
  other arithmetic  0.59 us (1%)
    ppermute x4, waiting for transfers between devices, plane_move(): return lax.ppermute(x, axes, pairs)  14.9 us
    pallas_call x7, Pallas kernels, fold(): pl.pallas_call(functools.partial(pair_kernel, (len(arrays), *plan)), out_...  14.1 us
    ppermute x4, starting transfers between devices, plane_move(): return lax.ppermute(x, axes, pairs)  10.9 us
    ppermute x7, starting transfers between devices, bulk_move(): return lax.ppermute(x, axes, pairs)  9.64 us
    ppermute x7, waiting for transfers between devices, bulk_move(): return lax.ppermute(x, axes, pairs)  4.43 us
    pallas_call x1, Pallas kernels, pack(): pl.pallas_call(pack_kernel, out_shape=jax.ShapeDtypeStruct((rows + KEYS,...  1.37 us
  transfers between devices with their start and end apart: 16, of which 7 were waited for; matrix products, arithmetic and copies ran while one was open for 0% of the time, Pallas kernels for 25%

profile of v4, /device:TPU:0, one launch (start us, length us, event | category | flops | bytes accessed | tf_op | source)
XLA Modules:
  0.0 56.4 jit_solution(2415266748912942809)
XLA Ops:
  0.0 1.4 %pack.1.refs_0_.refs_3_.refs_1_ = bf16[528,768]{1,0:T(8,128)(2,1)S(1)} custom-call(bf16[512,768]{1,0:T(8,128)(2,1)} %values_ref.1, s32[1,512]{1,0:T(1,128)} %bitcast.11, s32[1,512]{1,0:T(1,128)} %bitcast.12), custom_call_target="tpu_custom_call" | custom-call | tf_op jit(solution)/shard_map/pack/pallas_call | solution.py:63
  1.4 5.1 %collective-permute-start.2 = (bf16[528,768]{1,0:T(8,128)(2,1)S(1)}, bf16[528,768]{1,0:T(8,128)(2,1)S(1)}, u32[]{:S(2)}, u32[]{:S(2)}) collective-permute-start(bf16[528,768]{1,0:T(8,128)(2,1)S(1)} %pack.1.refs_0_.refs_3_.refs_1_), channel_id=1, source_target_pairs={{0,6},{1,7},{2,0},{3,1},{4,2},{5,3},{6,4},{7,5},{8,14},{9,15},{10,... | collective-permute-start | bytes 2433032 | tf_op jit(solution)/shard_map/ppermute | solution.py:178
  6.5 1.5 %collective-permute-start.7 = (bf16[528,768]{1,0:T(8,128)(2,1)S(1)}, bf16[528,768]{1,0:T(8,128)(2,1)S(1)}, u32[]{:S(2)}, u32[]{:S(2)}) collective-permute-start(bf16[528,768]{1,0:T(8,128)(2,1)S(1)} %pack.1.refs_0_.refs_3_.refs_1_), channel_id=1, source_target_pairs={{0,16},{1,17},{2,18},{3,19},{4,20},{5,21},{6,22},{7,23},{8,24},{9,... | collective-permute-start | bytes 2433032 | tf_op jit(solution)/shard_map/ppermute | solution.py:168
  8.0 1.5 %collective-permute-start.5 = (bf16[528,768]{1,0:T(8,128)(2,1)S(1)}, bf16[528,768]{1,0:T(8,128)(2,1)S(1)}, u32[]{:S(2)}, u32[]{:S(2)}) collective-permute-start(bf16[528,768]{1,0:T(8,128)(2,1)S(1)} %pack.1.refs_0_.refs_3_.refs_1_), channel_id=1, source_target_pairs={{0,8},{1,9},{2,10},{3,11},{4,12},{5,13},{6,14},{7,15},{8,0},{9,1},... | collective-permute-start | bytes 2433032 | tf_op jit(solution)/shard_map/ppermute | solution.py:168
  9.5 0.0 collective-permute-start.1
  9.5 1.4 %collective-permute-start = (bf16[528,768]{1,0:T(8,128)(2,1)S(1)}, bf16[528,768]{1,0:T(8,128)(2,1)S(1)}, u32[]{:S(2)}, u32[]{:S(2)}) collective-permute-start(bf16[528,768]{1,0:T(8,128)(2,1)S(1)} %pack.1.refs_0_.refs_3_.refs_1_), channel_id=1, source_target_pairs={{0,4},{1,5},{6,2},{7,3},{8,12},{9,13},{14,10},{15,11},{16,20},{17,... | collective-permute-start | bytes 2433032 | tf_op jit(solution)/shard_map/ppermute | solution.py:178
  10.9 14.1 %collective-permute-done.2.refs_0_.refs_2_ = bf16[528,768]{1,0:T(8,128)(2,1)S(1)} collective-permute-done((bf16[528,768]{1,0:T(8,128)(2,1)S(1)}, bf16[528,768]{1,0:T(8,128)(2,1)S(1)}, u32[]{:S(2)}, u32[]{:S(2)}) %collective-permute-start.2) | collective-permute-done | bytes 811040 | tf_op jit(solution)/shard_map/ppermute | solution.py:178
  25.0 0.1 collective-permute-start.3
  25.1 0.9 %collective-permute-done.7.refs_2_.refs_5_.refs_3_ = bf16[528,768]{1,0:T(8,128)(2,1)S(1)} collective-permute-done((bf16[528,768]{1,0:T(8,128)(2,1)S(1)}, bf16[528,768]{1,0:T(8,128)(2,1)S(1)}, u32[]{:S(2)}, u32[]{:S(2)}) %collective-permute-start.7) | collective-permute-done | bytes 811040 | tf_op jit(solution)/shard_map/ppermute | solution.py:168
  26.0 1.6 %collective-permute-start.8 = (bf16[272,768]{1,0:T(8,128)(2,1)S(1)}, bf16[272,768]{1,0:T(8,128)(2,1)S(1)}, u32[]{:S(2)}, u32[]{:S(2)}) collective-permute-start(bf16[272,768]{1,0:T(8,128)(2,1)S(1)} %slice.55), channel_id=1, source_target_pairs={{0,8},{1,9},{2,10},{3,11},{4,12},{5,13},{6,14},{7,15},{8,0},{9,1},... | collective-permute-start | bytes 1253384 | tf_op jit(solution)/shard_map/ppermute | solution.py:168
  27.6 1.6 %collective-permute-start.6 = (bf16[256,768]{1,0:T(8,128)(2,1)S(1)}, bf16[256,768]{1,0:T(8,128)(2,1)S(1)}, u32[]{:S(2)}, u32[]{:S(2)}) collective-permute-start(bf16[256,768]{1,0:T(8,128)(2,1)S(1)} %slice.54), channel_id=1, source_target_pairs={{0,16},{1,17},{2,18},{3,19},{4,20},{5,21},{6,22},{7,23},{8,24},{9,... | collective-permute-start | bytes 1179656 | tf_op jit(solution)/shard_map/ppermute | solution.py:168
  29.2 0.1 collective-permute-start.4
  29.3 1.3 %own.1.refs_3_ = f32[16,512]{1,0:T(8,128)S(1)} custom-call(bf16[528,768]{1,0:T(8,128)(2,1)S(1)} %pack.1.refs_0_.refs_3_.refs_1_, bf16[528,768]{1,0:T(8,128)(2,1)S(1)} %collective-permute-done.1.refs_1_, f32[16,512]{1,0:T(8,128)S(1)} %broadcast_in_dim.3.refs_2_), custom_call_target="tpu_custom_call" | custom-call | tf_op jit(solution)/shard_map/own/pallas_call | solution.py:147
  30.7 1.3 %near.2.refs_3_ = f32[16,512]{1,0:T(8,128)S(1)} custom-call(bf16[528,768]{1,0:T(8,128)(2,1)S(1)} %pack.1.refs_0_.refs_3_.refs_1_, bf16[528,768]{1,0:T(8,128)(2,1)S(1)} %collective-permute-done.1.refs_1_, bf16[528,768]{1,0:T(8,128)(2,1)S(1)} %collective-permute-done.5.refs_2_.refs_4_, f32[16,512]{1,0:T(8,128)S(1)} %own.1.refs_3_), custom_call_target="tpu_custom_call" | custom-call | tf_op jit(solution)/shard_map/near/pallas_call | solution.py:147
  32.0 1.3 %near.3.refs_6_ = f32[16,512]{1,0:T(8,128)S(1)} custom-call(bf16[528,768]{1,0:T(8,128)(2,1)S(1)} %pack.1.refs_0_.refs_3_.refs_1_, bf16[528,768]{1,0:T(8,128)(2,1)S(1)} %collective-permute-done.1.refs_1_, bf16[528,768]{1,0:T(8,128)(2,1)S(1)} %collective-permute-done.7.refs_2_.refs_5_.refs_3_, f32[16,512]{1,0:T(8,128)S(1)} %near.2.refs_3_), custom_call_target="tpu_custom_call" | custom-call | tf_op jit(solution)/shard_map/near/pallas_call | solution.py:147
  33.3 0.0 collective-permute-done.3.refs_1_.refs_3_
  33.3 3.4 %column.1.refs_7_ = f32[16,512]{1,0:T(8,128)S(1)} custom-call(bf16[528,768]{1,0:T(8,128)(2,1)S(1)} %collective-permute-done.2.refs_0_.refs_2_, bf16[336,768]{1,0:T(8,128)(2,1)S(1)} %collective-permute-done.3.refs_1_.refs_3_, bf16[192,768]{1,0:T(8,128)(2,1)S(1)} %collective-permute-done.4.refs_2_.refs_4_, bf16[528,768]{1,0:T(8,128)(2,1)S(1)} %pack.1.refs_0_.refs_3_.refs_1_, ...), custom_call_target="tpu_custom_call" | custom-call | tf_op jit(solution)/shard_map/column/pallas_call | solution.py:147
  36.7 1.3 %collective-permute-done.6.refs_5_.refs_4_ = bf16[256,768]{1,0:T(8,128)(2,1)S(1)} collective-permute-done((bf16[256,768]{1,0:T(8,128)(2,1)S(1)}, bf16[256,768]{1,0:T(8,128)(2,1)S(1)}, u32[]{:S(2)}, u32[]{:S(2)}) %collective-permute-start.6) | collective-permute-done | bytes 393248 | tf_op jit(solution)/shard_map/ppermute | solution.py:168
  38.0 2.3 %far.1.refs_6_ = f32[16,512]{1,0:T(8,128)S(1)} custom-call(bf16[528,768]{1,0:T(8,128)(2,1)S(1)} %pack.1.refs_0_.refs_3_.refs_1_, bf16[528,768]{1,0:T(8,128)(2,1)S(1)} %collective-permute-done.1.refs_1_, bf16[528,768]{1,0:T(8,128)(2,1)S(1)} %collective-permute-done.2.refs_0_.refs_2_, bf16[336,768]{1,0:T(8,128)(2,1)S(1)} %collective-permute-done.3.refs_1_.refs_3_, ...), custom_call_target="tpu_custom_call" | custom-call | tf_op jit(solution)/shard_map/far/pallas_call | solution.py:147
  40.3 0.8 %collective-permute-done.refs_0_ = bf16[528,768]{1,0:T(8,128)(2,1)S(1)} collective-permute-done((bf16[528,768]{1,0:T(8,128)(2,1)S(1)}, bf16[528,768]{1,0:T(8,128)(2,1)S(1)}, u32[]{:S(2)}, u32[]{:S(2)}) %collective-permute-start) | collective-permute-done | bytes 811040 | tf_op jit(solution)/shard_map/ppermute | solution.py:178
  41.2 1.7 %collective-permute-start.10 = (f32[2,512]{1,0:T(2,128)S(1)}, f32[2,512]{1,0:T(2,128)S(1)}, u32[]{:S(2)}, u32[]{:S(2)}) collective-permute-start(f32[2,512]{1,0:T(2,128)S(1)} %slice.57), channel_id=1, source_target_pairs={{0,2},{1,3},{2,4},{3,5},{4,6},{5,7},{6,0},{7,1},{8,10},{9,11},{10,... | collective-permute-start | bytes 12296 | tf_op jit(solution)/shard_map/ppermute | solution.py:178
  42.9 2.2 %last.1.refs_6_ = f32[16,512]{1,0:T(8,128)S(1)} custom-call(bf16[528,768]{1,0:T(8,128)(2,1)S(1)} %collective-permute-done.refs_0_, bf16[528,768]{1,0:T(8,128)(2,1)S(1)} %pack.1.refs_0_.refs_3_.refs_1_, bf16[528,768]{1,0:T(8,128)(2,1)S(1)} %collective-permute-done.5.refs_2_.refs_4_, bf16[528,768]{1,0:T(8,128)(2,1)S(1)} %collective-permute-done.7.refs_2_.refs_5_.refs_3_, ...), custom_call_target="tpu_custom_call" | custom-call | tf_op jit(solution)/shard_map/last/pallas_call | solution.py:147
  45.1 2.2 %rest.1 = f32[16,512]{1,0:T(8,128)S(1)} custom-call(bf16[528,768]{1,0:T(8,128)(2,1)S(1)} %collective-permute-done.9.refs_0_, bf16[528,768]{1,0:T(8,128)(2,1)S(1)} %pack.1.refs_0_.refs_3_.refs_1_, bf16[528,768]{1,0:T(8,128)(2,1)S(1)} %collective-permute-done.5.refs_2_.refs_4_, bf16[528,768]{1,0:T(8,128)(2,1)S(1)} %collective-permute-done.7.refs_2_.refs_5_.refs_3_, ...), custom_call_target="tpu_custom_call" | custom-call | tf_op jit(solution)/shard_map/rest/pallas_call | solution.py:147
  47.3 2.7 %collective-permute-start.11 = (f32[2,512]{1,0:T(2,128)S(1)}, f32[2,512]{1,0:T(2,128)S(1)}, u32[]{:S(2)}, u32[]{:S(2)}) collective-permute-start(f32[2,512]{1,0:T(2,128)S(1)} %slice.58), channel_id=1, source_target_pairs={{0,4},{1,5},{2,6},{3,7},{4,0},{5,1},{6,2},{7,3},{8,12},{9,13},{10,... | collective-permute-start | bytes 12296 | tf_op jit(solution)/shard_map/ppermute | solution.py:178
  50.0 1.7 %collective-permute-start.15 = (f32[16,512]{1,0:T(8,128)S(1)}, f32[16,512]{1,0:T(8,128)S(1)}, u32[]{:S(2)}, u32[]{:S(2)}) collective-permute-start(f32[16,512]{1,0:T(8,128)S(1)} %rest.1), channel_id=1, source_target_pairs={{0,24},{1,25},{2,26},{3,27},{4,28},{5,29},{6,30},{7,31},{8,16},{9,... | collective-permute-start | bytes 98312 | tf_op jit(solution)/shard_map/ppermute | solution.py:168
  51.7 0.5 collective-permute-start.14
  52.2 1.2 %collective-permute-start.13 = (f32[512]{0:T(512)S(1)}, f32[512]{0:T(512)S(1)}, u32[]{:S(2)}, u32[]{:S(2)}) collective-permute-start(f32[512]{0:T(512)S(1)} %bitcast.13), channel_id=1, source_target_pairs={{0,8},{1,9},{2,10},{3,11},{4,12},{5,13},{6,14},{7,15},{8,0},{9,1},... | collective-permute-start | bytes 6152 | tf_op jit(solution)/shard_map/ppermute | solution.py:168
  53.5 0.1 collective-permute-start.12
  53.6 1.2 %collective-permute-done.15 = f32[16,512]{1,0:T(8,128)S(1)} collective-permute-done((f32[16,512]{1,0:T(8,128)S(1)}, f32[16,512]{1,0:T(8,128)S(1)}, u32[]{:S(2)}, u32[]{:S(2)}) %collective-permute-start.15) | collective-permute-done | bytes 32800 | tf_op jit(solution)/shard_map/ppermute | solution.py:168
  54.8 0.5 collective-permute-done.14
  55.3 0.5 collective-permute-done.13
  55.8 0.6 %maximum_maximum_fusion = f32[512]{0:T(512)} fusion(f32[512]{0:T(512)S(1)} %bitcast.8, f32[512]{0:T(512)S(1)} %collective-permute-done.14, f32[512]{0:T(512)S(1)} %bitcast.9, f32[512]{0:T(512)S(1)} %collective-permute-done.13, f32[512]{0:T(512)S(1)} %bitcast.10, f32[512]{0:T(512)S(1)} %collective-permute-done.12), kind=kLoop, calls=%fused_computation.2 | loop fusion | flops 2560 | bytes 14336 | tf_op jit(solution)/shard_map/max | solution.py:240
  (20 shorter events, 0.2 us)
Async XLA Ops:
  1.4 23.6 %collective-permute-start.2 = (bf16[528,768]{1,0:T(8,128)(2,1)S(1)}, bf16[528,768]{1,0:T(8,128)(2,1)S(1)}, u32[]{:S(2)}, u32[]{:S(2)}) collective-permute-start(bf16[528,768]{1,0:T(8,128)(2,1)S(1)} %pack.1.refs_0_.refs_3_.refs_1_), channel_id=1, source_target_pairs={{0,6},{1,7},{2,0},{3,1},{4,2},{5,3},{6,4},{7,5},{8,14},{9,15},{10,... | collective-permute-start | bytes 2433032 | tf_op jit(solution)/shard_map/ppermute | solution.py:178
  6.5 19.5 %collective-permute-start.7 = (bf16[528,768]{1,0:T(8,128)(2,1)S(1)}, bf16[528,768]{1,0:T(8,128)(2,1)S(1)}, u32[]{:S(2)}, u32[]{:S(2)}) collective-permute-start(bf16[528,768]{1,0:T(8,128)(2,1)S(1)} %pack.1.refs_0_.refs_3_.refs_1_), channel_id=1, source_target_pairs={{0,16},{1,17},{2,18},{3,19},{4,20},{5,21},{6,22},{7,23},{8,24},{9,... | collective-permute-start | bytes 2433032 | tf_op jit(solution)/shard_map/ppermute | solution.py:168
  8.0 19.6 %collective-permute-start.5 = (bf16[528,768]{1,0:T(8,128)(2,1)S(1)}, bf16[528,768]{1,0:T(8,128)(2,1)S(1)}, u32[]{:S(2)}, u32[]{:S(2)}) collective-permute-start(bf16[528,768]{1,0:T(8,128)(2,1)S(1)} %pack.1.refs_0_.refs_3_.refs_1_), channel_id=1, source_target_pairs={{0,8},{1,9},{2,10},{3,11},{4,12},{5,13},{6,14},{7,15},{8,0},{9,1},... | collective-permute-start | bytes 2433032 | tf_op jit(solution)/shard_map/ppermute | solution.py:168
  9.5 19.8 %collective-permute-start.1 = (bf16[528,768]{1,0:T(8,128)(2,1)S(1)}, bf16[528,768]{1,0:T(8,128)(2,1)S(1)}, u32[]{:S(2)}, u32[]{:S(2)}) collective-permute-start(bf16[528,768]{1,0:T(8,128)(2,1)S(1)} %pack.1.refs_0_.refs_3_.refs_1_), channel_id=1, source_target_pairs={{0,1},{1,0},{2,3},{3,2},{4,5},{5,4},{6,7},{7,6},{8,9},{9,8},{10,11... | collective-permute-start | bytes 2433032 | tf_op jit(solution)/shard_map/ppermute | solution.py:172
  9.5 31.7 %collective-permute-start = (bf16[528,768]{1,0:T(8,128)(2,1)S(1)}, bf16[528,768]{1,0:T(8,128)(2,1)S(1)}, u32[]{:S(2)}, u32[]{:S(2)}) collective-permute-start(bf16[528,768]{1,0:T(8,128)(2,1)S(1)} %pack.1.refs_0_.refs_3_.refs_1_), channel_id=1, source_target_pairs={{0,4},{1,5},{6,2},{7,3},{8,12},{9,13},{14,10},{15,11},{16,20},{17,... | collective-permute-start | bytes 2433032 | tf_op jit(solution)/shard_map/ppermute | solution.py:178
  25.0 8.3 %collective-permute-start.3 = (bf16[336,768]{1,0:T(8,128)(2,1)S(1)}, bf16[336,768]{1,0:T(8,128)(2,1)S(1)}, u32[]{:S(2)}, u32[]{:S(2)}) collective-permute-start(bf16[336,768]{1,0:T(8,128)(2,1)S(1)} %slice.52), channel_id=1, source_target_pairs={{0,1},{1,0},{2,3},{3,2},{4,5},{5,4},{6,7},{7,6},{8,9},{9,8},{10,11... | collective-permute-start | bytes 1548296 | tf_op jit(solution)/shard_map/ppermute | solution.py:172
  26.0 12.0 %collective-permute-start.8 = (bf16[272,768]{1,0:T(8,128)(2,1)S(1)}, bf16[272,768]{1,0:T(8,128)(2,1)S(1)}, u32[]{:S(2)}, u32[]{:S(2)}) collective-permute-start(bf16[272,768]{1,0:T(8,128)(2,1)S(1)} %slice.55), channel_id=1, source_target_pairs={{0,8},{1,9},{2,10},{3,11},{4,12},{5,13},{6,14},{7,15},{8,0},{9,1},... | collective-permute-start | bytes 1253384 | tf_op jit(solution)/shard_map/ppermute | solution.py:168
  27.6 10.4 %collective-permute-start.6 = (bf16[256,768]{1,0:T(8,128)(2,1)S(1)}, bf16[256,768]{1,0:T(8,128)(2,1)S(1)}, u32[]{:S(2)}, u32[]{:S(2)}) collective-permute-start(bf16[256,768]{1,0:T(8,128)(2,1)S(1)} %slice.54), channel_id=1, source_target_pairs={{0,16},{1,17},{2,18},{3,19},{4,20},{5,21},{6,22},{7,23},{8,24},{9,... | collective-permute-start | bytes 1179656 | tf_op jit(solution)/shard_map/ppermute | solution.py:168
  29.2 4.0 %collective-permute-start.4 = (bf16[192,768]{1,0:T(8,128)(2,1)S(1)}, bf16[192,768]{1,0:T(8,128)(2,1)S(1)}, u32[]{:S(2)}, u32[]{:S(2)}) collective-permute-start(bf16[192,768]{1,0:T(8,128)(2,1)S(1)} %slice.53), channel_id=1, source_target_pairs={{0,1},{1,0},{2,3},{3,2},{4,5},{5,4},{6,7},{7,6},{8,9},{9,8},{10,11... | collective-permute-start | bytes 884744 | tf_op jit(solution)/shard_map/ppermute | solution.py:172
  41.2 3.9 %collective-permute-start.9 = (bf16[528,768]{1,0:T(8,128)(2,1)S(1)}, bf16[528,768]{1,0:T(8,128)(2,1)S(1)}, u32[]{:S(2)}, u32[]{:S(2)}) collective-permute-start(bf16[528,768]{1,0:T(8,128)(2,1)S(1)} %collective-permute-done.refs_0_), channel_id=1, source_target_pairs={{0,1},{1,0},{2,3},{3,2},{4,5},{5,4},{6,7},{7,6},{8,9},{9,8},{10,11... | collective-permute-start | bytes 2433032 | tf_op jit(solution)/shard_map/ppermute | solution.py:172
  41.2 12.3 %collective-permute-start.10 = (f32[2,512]{1,0:T(2,128)S(1)}, f32[2,512]{1,0:T(2,128)S(1)}, u32[]{:S(2)}, u32[]{:S(2)}) collective-permute-start(f32[2,512]{1,0:T(2,128)S(1)} %slice.57), channel_id=1, source_target_pairs={{0,2},{1,3},{2,4},{3,5},{4,6},{5,7},{6,0},{7,1},{8,10},{9,11},{10,... | collective-permute-start | bytes 12296 | tf_op jit(solution)/shard_map/ppermute | solution.py:178
  47.3 6.2 %collective-permute-start.11 = (f32[2,512]{1,0:T(2,128)S(1)}, f32[2,512]{1,0:T(2,128)S(1)}, u32[]{:S(2)}, u32[]{:S(2)}) collective-permute-start(f32[2,512]{1,0:T(2,128)S(1)} %slice.58), channel_id=1, source_target_pairs={{0,4},{1,5},{2,6},{3,7},{4,0},{5,1},{6,2},{7,3},{8,12},{9,13},{10,... | collective-permute-start | bytes 12296 | tf_op jit(solution)/shard_map/ppermute | solution.py:178
  50.0 4.8 %collective-permute-start.15 = (f32[16,512]{1,0:T(8,128)S(1)}, f32[16,512]{1,0:T(8,128)S(1)}, u32[]{:S(2)}, u32[]{:S(2)}) collective-permute-start(f32[16,512]{1,0:T(8,128)S(1)} %rest.1), channel_id=1, source_target_pairs={{0,24},{1,25},{2,26},{3,27},{4,28},{5,29},{6,30},{7,31},{8,16},{9,... | collective-permute-start | bytes 98312 | tf_op jit(solution)/shard_map/ppermute | solution.py:168
  51.7 3.6 %collective-permute-start.14 = (f32[512]{0:T(512)S(1)}, f32[512]{0:T(512)S(1)}, u32[]{:S(2)}, u32[]{:S(2)}) collective-permute-start(f32[512]{0:T(512)S(1)} %bitcast.14), channel_id=1, source_target_pairs={{0,16},{1,17},{2,18},{3,19},{4,20},{5,21},{6,22},{7,23},{8,24},{9,... | collective-permute-start | bytes 6152 | tf_op jit(solution)/shard_map/ppermute | solution.py:168
  52.2 3.6 %collective-permute-start.13 = (f32[512]{0:T(512)S(1)}, f32[512]{0:T(512)S(1)}, u32[]{:S(2)}, u32[]{:S(2)}) collective-permute-start(f32[512]{0:T(512)S(1)} %bitcast.13), channel_id=1, source_target_pairs={{0,8},{1,9},{2,10},{3,11},{4,12},{5,13},{6,14},{7,15},{8,0},{9,1},... | collective-permute-start | bytes 6152 | tf_op jit(solution)/shard_map/ppermute | solution.py:168
  53.5 2.3 %collective-permute-start.12 = (f32[512]{0:T(512)S(1)}, f32[512]{0:T(512)S(1)}, u32[]{:S(2)}, u32[]{:S(2)}) collective-permute-start(f32[512]{0:T(512)S(1)} %bitcast.15), channel_id=1, source_target_pairs={{0,1},{1,0},{2,3},{3,2},{4,5},{5,4},{6,7},{7,6},{8,9},{9,8},{10,11... | collective-permute-start | bytes 6152 | tf_op jit(solution)/shard_map/ppermute | solution.py:172

commit v5 on v3

--- a/solution.py
+++ b/solution.py
@@ -223,7 +223,7 @@
     best = fold(best, most, blocks + near, "column")
     best = fold(best, same + most, far, "far")
 
-    parts = [go_home(best[z_line(r) : tz_line(r) + 1], r) for r in range(k)]
+    parts = [go_home(best, r)[z_line(r) : tz_line(r) + 1] for r in range(k)]
     blocks += near + far
     z_last = after(z[k], best)
     z_last_twin = core_move(z_last)

time: 56.7 us -> 56.6 us (level)
  no operation moved by 1% of the time
where the time goes in v5:
time: 56.6 us; the launch traced here: 56.4 us
  starting transfers between devices  20.7 us (37%)
  waiting for transfers between devices  19.8 us (35%)
  Pallas kernels  15.1 us (27%)
  other arithmetic  0.59 us (1%)
    ppermute x4, waiting for transfers between devices, plane_move(): return lax.ppermute(x, axes, pairs)  14.9 us
    pallas_call x6, Pallas kernels, fold(): pl.pallas_call(functools.partial(pair_kernel, (len(arrays), *plan)), out_...  13.6 us
    ppermute x4, starting transfers between devices, plane_move(): return lax.ppermute(x, axes, pairs)  10.9 us
    ppermute x7, starting transfers between devices, bulk_move(): return lax.ppermute(x, axes, pairs)  9.64 us
    ppermute x7, waiting for transfers between devices, bulk_move(): return lax.ppermute(x, axes, pairs)  4.84 us
    pallas_call x1, Pallas kernels, pack(): pl.pallas_call(pack_kernel, out_shape=jax.ShapeDtypeStruct((rows + KEYS,...  1.5 us
  transfers between devices with their start and end apart: 16, of which 7 were waited for; matrix products, arithmetic and copies ran while one was open for 0% of the time, Pallas kernels for 24%

profile of v5, /device:TPU:0, one launch (start us, length us, event | category | flops | bytes accessed | tf_op | source)
XLA Modules:
  0.0 56.4 jit_solution(9421807377533535934)
XLA Ops:
  0.0 1.5 %pack.1.refs_0_.refs_3_.refs_1_ = bf16[528,768]{1,0:T(8,128)(2,1)S(1)} custom-call(bf16[512,768]{1,0:T(8,128)(2,1)} %values_ref.1, s32[1,512]{1,0:T(1,128)} %bitcast.11, s32[1,512]{1,0:T(1,128)} %bitcast.12), custom_call_target="tpu_custom_call" | custom-call | tf_op jit(solution)/shard_map/pack/pallas_call | solution.py:63
  1.5 5.1 %collective-permute-start.2 = (bf16[528,768]{1,0:T(8,128)(2,1)S(1)}, bf16[528,768]{1,0:T(8,128)(2,1)S(1)}, u32[]{:S(2)}, u32[]{:S(2)}) collective-permute-start(bf16[528,768]{1,0:T(8,128)(2,1)S(1)} %pack.1.refs_0_.refs_3_.refs_1_), channel_id=1, source_target_pairs={{0,6},{1,7},{2,0},{3,1},{4,2},{5,3},{6,4},{7,5},{8,14},{9,15},{10,... | collective-permute-start | bytes 2433032 | tf_op jit(solution)/shard_map/ppermute | solution.py:178
  6.6 1.5 %collective-permute-start.7 = (bf16[528,768]{1,0:T(8,128)(2,1)S(1)}, bf16[528,768]{1,0:T(8,128)(2,1)S(1)}, u32[]{:S(2)}, u32[]{:S(2)}) collective-permute-start(bf16[528,768]{1,0:T(8,128)(2,1)S(1)} %pack.1.refs_0_.refs_3_.refs_1_), channel_id=1, source_target_pairs={{0,16},{1,17},{2,18},{3,19},{4,20},{5,21},{6,22},{7,23},{8,24},{9,... | collective-permute-start | bytes 2433032 | tf_op jit(solution)/shard_map/ppermute | solution.py:168
  8.1 1.5 %collective-permute-start.5 = (bf16[528,768]{1,0:T(8,128)(2,1)S(1)}, bf16[528,768]{1,0:T(8,128)(2,1)S(1)}, u32[]{:S(2)}, u32[]{:S(2)}) collective-permute-start(bf16[528,768]{1,0:T(8,128)(2,1)S(1)} %pack.1.refs_0_.refs_3_.refs_1_), channel_id=1, source_target_pairs={{0,8},{1,9},{2,10},{3,11},{4,12},{5,13},{6,14},{7,15},{8,0},{9,1},... | collective-permute-start | bytes 2433032 | tf_op jit(solution)/shard_map/ppermute | solution.py:168
  9.6 0.0 collective-permute-start.1
  9.6 1.4 %collective-permute-start = (bf16[528,768]{1,0:T(8,128)(2,1)S(1)}, bf16[528,768]{1,0:T(8,128)(2,1)S(1)}, u32[]{:S(2)}, u32[]{:S(2)}) collective-permute-start(bf16[528,768]{1,0:T(8,128)(2,1)S(1)} %pack.1.refs_0_.refs_3_.refs_1_), channel_id=1, source_target_pairs={{0,4},{1,5},{6,2},{7,3},{8,12},{9,13},{14,10},{15,11},{16,20},{17,... | collective-permute-start | bytes 2433032 | tf_op jit(solution)/shard_map/ppermute | solution.py:178
  11.0 14.1 %collective-permute-done.2.refs_0_.refs_2_ = bf16[528,768]{1,0:T(8,128)(2,1)S(1)} collective-permute-done((bf16[528,768]{1,0:T(8,128)(2,1)S(1)}, bf16[528,768]{1,0:T(8,128)(2,1)S(1)}, u32[]{:S(2)}, u32[]{:S(2)}) %collective-permute-start.2) | collective-permute-done | bytes 811040 | tf_op jit(solution)/shard_map/ppermute | solution.py:178
  25.1 0.1 collective-permute-start.3
  25.2 0.9 %collective-permute-done.7.refs_3_.refs_5_ = bf16[528,768]{1,0:T(8,128)(2,1)S(1)} collective-permute-done((bf16[528,768]{1,0:T(8,128)(2,1)S(1)}, bf16[528,768]{1,0:T(8,128)(2,1)S(1)}, u32[]{:S(2)}, u32[]{:S(2)}) %collective-permute-start.7) | collective-permute-done | bytes 811040 | tf_op jit(solution)/shard_map/ppermute | solution.py:168
  26.2 1.6 %collective-permute-start.8 = (bf16[272,768]{1,0:T(8,128)(2,1)S(1)}, bf16[272,768]{1,0:T(8,128)(2,1)S(1)}, u32[]{:S(2)}, u32[]{:S(2)}) collective-permute-start(bf16[272,768]{1,0:T(8,128)(2,1)S(1)} %slice.55), channel_id=1, source_target_pairs={{0,8},{1,9},{2,10},{3,11},{4,12},{5,13},{6,14},{7,15},{8,0},{9,1},... | collective-permute-start | bytes 1253384 | tf_op jit(solution)/shard_map/ppermute | solution.py:168
  27.7 0.0 collective-permute-done.5.refs_2_.refs_4_
  27.8 1.6 %collective-permute-start.6 = (bf16[256,768]{1,0:T(8,128)(2,1)S(1)}, bf16[256,768]{1,0:T(8,128)(2,1)S(1)}, u32[]{:S(2)}, u32[]{:S(2)}) collective-permute-start(bf16[256,768]{1,0:T(8,128)(2,1)S(1)} %slice.54), channel_id=1, source_target_pairs={{0,16},{1,17},{2,18},{3,19},{4,20},{5,21},{6,22},{7,23},{8,24},{9,... | collective-permute-start | bytes 1179656 | tf_op jit(solution)/shard_map/ppermute | solution.py:168
  29.4 0.0 collective-permute-done.1.refs_1_
  29.4 0.1 collective-permute-start.4
  29.5 1.3 %own.1.refs_4_ = f32[16,512]{1,0:T(8,128)S(1)} custom-call(bf16[528,768]{1,0:T(8,128)(2,1)S(1)} %pack.1.refs_0_.refs_3_.refs_1_, bf16[528,768]{1,0:T(8,128)(2,1)S(1)} %collective-permute-done.1.refs_1_, f32[16,512]{1,0:T(8,128)S(1)} %broadcast_in_dim.3.refs_2_), custom_call_target="tpu_custom_call" | custom-call | tf_op jit(solution)/shard_map/own/pallas_call | solution.py:147
  30.8 2.1 %near.1.refs_6_ = f32[16,512]{1,0:T(8,128)S(1)} custom-call(bf16[528,768]{1,0:T(8,128)(2,1)S(1)} %pack.1.refs_0_.refs_3_.refs_1_, bf16[528,768]{1,0:T(8,128)(2,1)S(1)} %collective-permute-done.1.refs_1_, bf16[528,768]{1,0:T(8,128)(2,1)S(1)} %collective-permute-done.5.refs_2_.refs_4_, bf16[528,768]{1,0:T(8,128)(2,1)S(1)} %collective-permute-done.7.refs_3_.refs_5_, ...), custom_call_target="tpu_custom_call" | custom-call | tf_op jit(solution)/shard_map/near/pallas_call | solution.py:147
  33.0 3.4 %column.1.refs_7_ = f32[16,512]{1,0:T(8,128)S(1)} custom-call(bf16[528,768]{1,0:T(8,128)(2,1)S(1)} %collective-permute-done.2.refs_0_.refs_2_, bf16[336,768]{1,0:T(8,128)(2,1)S(1)} %collective-permute-done.3.refs_1_.refs_3_, bf16[192,768]{1,0:T(8,128)(2,1)S(1)} %collective-permute-done.4.refs_2_.refs_4_, bf16[528,768]{1,0:T(8,128)(2,1)S(1)} %pack.1.refs_0_.refs_3_.refs_1_, ...), custom_call_target="tpu_custom_call" | custom-call | tf_op jit(solution)/shard_map/column/pallas_call | solution.py:147
  36.4 1.7 %collective-permute-done.6.refs_5_.refs_4_ = bf16[256,768]{1,0:T(8,128)(2,1)S(1)} collective-permute-done((bf16[256,768]{1,0:T(8,128)(2,1)S(1)}, bf16[256,768]{1,0:T(8,128)(2,1)S(1)}, u32[]{:S(2)}, u32[]{:S(2)}) %collective-permute-start.6) | collective-permute-done | bytes 393248 | tf_op jit(solution)/shard_map/ppermute | solution.py:168
  38.1 2.3 %far.1.refs_6_ = f32[16,512]{1,0:T(8,128)S(1)} custom-call(bf16[528,768]{1,0:T(8,128)(2,1)S(1)} %pack.1.refs_0_.refs_3_.refs_1_, bf16[528,768]{1,0:T(8,128)(2,1)S(1)} %collective-permute-done.1.refs_1_, bf16[528,768]{1,0:T(8,128)(2,1)S(1)} %collective-permute-done.2.refs_0_.refs_2_, bf16[336,768]{1,0:T(8,128)(2,1)S(1)} %collective-permute-done.3.refs_1_.refs_3_, ...), custom_call_target="tpu_custom_call" | custom-call | tf_op jit(solution)/shard_map/far/pallas_call | solution.py:147
  40.5 0.8 %collective-permute-done.refs_0_ = bf16[528,768]{1,0:T(8,128)(2,1)S(1)} collective-permute-done((bf16[528,768]{1,0:T(8,128)(2,1)S(1)}, bf16[528,768]{1,0:T(8,128)(2,1)S(1)}, u32[]{:S(2)}, u32[]{:S(2)}) %collective-permute-start) | collective-permute-done | bytes 811040 | tf_op jit(solution)/shard_map/ppermute | solution.py:178
  41.3 1.5 %collective-permute-start.10 = (f32[16,512]{1,0:T(8,128)S(1)}, f32[16,512]{1,0:T(8,128)S(1)}, u32[]{:S(2)}, u32[]{:S(2)}) collective-permute-start(f32[16,512]{1,0:T(8,128)S(1)} %far.1.refs_6_), channel_id=1, source_target_pairs={{0,2},{1,3},{2,4},{3,5},{4,6},{5,7},{6,0},{7,1},{8,10},{9,11},{10,... | collective-permute-start | bytes 98312 | tf_op jit(solution)/shard_map/ppermute | solution.py:178
  42.8 2.2 %last.1.refs_6_ = f32[16,512]{1,0:T(8,128)S(1)} custom-call(bf16[528,768]{1,0:T(8,128)(2,1)S(1)} %collective-permute-done.refs_0_, bf16[528,768]{1,0:T(8,128)(2,1)S(1)} %pack.1.refs_0_.refs_3_.refs_1_, bf16[528,768]{1,0:T(8,128)(2,1)S(1)} %collective-permute-done.5.refs_2_.refs_4_, bf16[528,768]{1,0:T(8,128)(2,1)S(1)} %collective-permute-done.7.refs_3_.refs_5_, ...), custom_call_target="tpu_custom_call" | custom-call | tf_op jit(solution)/shard_map/last/pallas_call | solution.py:147
  45.0 2.2 %rest.1 = f32[16,512]{1,0:T(8,128)S(1)} custom-call(bf16[528,768]{1,0:T(8,128)(2,1)S(1)} %collective-permute-done.9.refs_0_, bf16[528,768]{1,0:T(8,128)(2,1)S(1)} %pack.1.refs_0_.refs_3_.refs_1_, bf16[528,768]{1,0:T(8,128)(2,1)S(1)} %collective-permute-done.5.refs_2_.refs_4_, bf16[528,768]{1,0:T(8,128)(2,1)S(1)} %collective-permute-done.7.refs_3_.refs_5_, ...), custom_call_target="tpu_custom_call" | custom-call | tf_op jit(solution)/shard_map/rest/pallas_call | solution.py:147
  47.2 2.9 %collective-permute-start.11 = (f32[2,512]{1,0:T(2,128)S(1)}, f32[2,512]{1,0:T(2,128)S(1)}, u32[]{:S(2)}, u32[]{:S(2)}) collective-permute-start(f32[2,512]{1,0:T(2,128)S(1)} %slice.58), channel_id=1, source_target_pairs={{0,4},{1,5},{2,6},{3,7},{4,0},{5,1},{6,2},{7,3},{8,12},{9,13},{10,... | collective-permute-start | bytes 12296 | tf_op jit(solution)/shard_map/ppermute | solution.py:178
  50.1 1.7 %collective-permute-start.15 = (f32[16,512]{1,0:T(8,128)S(1)}, f32[16,512]{1,0:T(8,128)S(1)}, u32[]{:S(2)}, u32[]{:S(2)}) collective-permute-start(f32[16,512]{1,0:T(8,128)S(1)} %rest.1), channel_id=1, source_target_pairs={{0,24},{1,25},{2,26},{3,27},{4,28},{5,29},{6,30},{7,31},{8,16},{9,... | collective-permute-start | bytes 98312 | tf_op jit(solution)/shard_map/ppermute | solution.py:168
  51.8 0.5 collective-permute-start.14
  52.3 1.3 %collective-permute-start.13 = (f32[512]{0:T(512)S(1)}, f32[512]{0:T(512)S(1)}, u32[]{:S(2)}, u32[]{:S(2)}) collective-permute-start(f32[512]{0:T(512)S(1)} %bitcast.13), channel_id=1, source_target_pairs={{0,8},{1,9},{2,10},{3,11},{4,12},{5,13},{6,14},{7,15},{8,0},{9,1},... | collective-permute-start | bytes 6152 | tf_op jit(solution)/shard_map/ppermute | solution.py:168
  53.6 0.1 collective-permute-start.12
  53.7 1.2 %collective-permute-done.15 = f32[16,512]{1,0:T(8,128)S(1)} collective-permute-done((f32[16,512]{1,0:T(8,128)S(1)}, f32[16,512]{1,0:T(8,128)S(1)}, u32[]{:S(2)}, u32[]{:S(2)}) %collective-permute-start.15) | collective-permute-done | bytes 32800 | tf_op jit(solution)/shard_map/ppermute | solution.py:168
  54.9 0.4 collective-permute-done.14
  55.3 0.5 collective-permute-done.13
  55.9 0.6 %maximum_maximum_fusion = f32[512]{0:T(512)} fusion(f32[512]{0:T(512)S(1)} %bitcast.8, f32[512]{0:T(512)S(1)} %collective-permute-done.14, f32[512]{0:T(512)S(1)} %bitcast.9, f32[512]{0:T(512)S(1)} %collective-permute-done.13, f32[512]{0:T(512)S(1)} %bitcast.10, f32[512]{0:T(512)S(1)} %collective-permute-done.12), kind=kLoop, calls=%fused_computation.2 | loop fusion | flops 2560 | bytes 14336 | tf_op jit(solution)/shard_map/max | solution.py:239
  (18 shorter events, 0.2 us)
Async XLA Ops:
  1.5 23.6 %collective-permute-start.2 = (bf16[528,768]{1,0:T(8,128)(2,1)S(1)}, bf16[528,768]{1,0:T(8,128)(2,1)S(1)}, u32[]{:S(2)}, u32[]{:S(2)}) collective-permute-start(bf16[528,768]{1,0:T(8,128)(2,1)S(1)} %pack.1.refs_0_.refs_3_.refs_1_), channel_id=1, source_target_pairs={{0,6},{1,7},{2,0},{3,1},{4,2},{5,3},{6,4},{7,5},{8,14},{9,15},{10,... | collective-permute-start | bytes 2433032 | tf_op jit(solution)/shard_map/ppermute | solution.py:178
  6.6 19.5 %collective-permute-start.7 = (bf16[528,768]{1,0:T(8,128)(2,1)S(1)}, bf16[528,768]{1,0:T(8,128)(2,1)S(1)}, u32[]{:S(2)}, u32[]{:S(2)}) collective-permute-start(bf16[528,768]{1,0:T(8,128)(2,1)S(1)} %pack.1.refs_0_.refs_3_.refs_1_), channel_id=1, source_target_pairs={{0,16},{1,17},{2,18},{3,19},{4,20},{5,21},{6,22},{7,23},{8,24},{9,... | collective-permute-start | bytes 2433032 | tf_op jit(solution)/shard_map/ppermute | solution.py:168
  8.1 19.6 %collective-permute-start.5 = (bf16[528,768]{1,0:T(8,128)(2,1)S(1)}, bf16[528,768]{1,0:T(8,128)(2,1)S(1)}, u32[]{:S(2)}, u32[]{:S(2)}) collective-permute-start(bf16[528,768]{1,0:T(8,128)(2,1)S(1)} %pack.1.refs_0_.refs_3_.refs_1_), channel_id=1, source_target_pairs={{0,8},{1,9},{2,10},{3,11},{4,12},{5,13},{6,14},{7,15},{8,0},{9,1},... | collective-permute-start | bytes 2433032 | tf_op jit(solution)/shard_map/ppermute | solution.py:168
  9.6 19.8 %collective-permute-start.1 = (bf16[528,768]{1,0:T(8,128)(2,1)S(1)}, bf16[528,768]{1,0:T(8,128)(2,1)S(1)}, u32[]{:S(2)}, u32[]{:S(2)}) collective-permute-start(bf16[528,768]{1,0:T(8,128)(2,1)S(1)} %pack.1.refs_0_.refs_3_.refs_1_), channel_id=1, source_target_pairs={{0,1},{1,0},{2,3},{3,2},{4,5},{5,4},{6,7},{7,6},{8,9},{9,8},{10,11... | collective-permute-start | bytes 2433032 | tf_op jit(solution)/shard_map/ppermute | solution.py:172
  9.6 31.7 %collective-permute-start = (bf16[528,768]{1,0:T(8,128)(2,1)S(1)}, bf16[528,768]{1,0:T(8,128)(2,1)S(1)}, u32[]{:S(2)}, u32[]{:S(2)}) collective-permute-start(bf16[528,768]{1,0:T(8,128)(2,1)S(1)} %pack.1.refs_0_.refs_3_.refs_1_), channel_id=1, source_target_pairs={{0,4},{1,5},{6,2},{7,3},{8,12},{9,13},{14,10},{15,11},{16,20},{17,... | collective-permute-start | bytes 2433032 | tf_op jit(solution)/shard_map/ppermute | solution.py:178
  25.1 7.8 %collective-permute-start.3 = (bf16[336,768]{1,0:T(8,128)(2,1)S(1)}, bf16[336,768]{1,0:T(8,128)(2,1)S(1)}, u32[]{:S(2)}, u32[]{:S(2)}) collective-permute-start(bf16[336,768]{1,0:T(8,128)(2,1)S(1)} %slice.52), channel_id=1, source_target_pairs={{0,1},{1,0},{2,3},{3,2},{4,5},{5,4},{6,7},{7,6},{8,9},{9,8},{10,11... | collective-permute-start | bytes 1548296 | tf_op jit(solution)/shard_map/ppermute | solution.py:172
  26.2 12.0 %collective-permute-start.8 = (bf16[272,768]{1,0:T(8,128)(2,1)S(1)}, bf16[272,768]{1,0:T(8,128)(2,1)S(1)}, u32[]{:S(2)}, u32[]{:S(2)}) collective-permute-start(bf16[272,768]{1,0:T(8,128)(2,1)S(1)} %slice.55), channel_id=1, source_target_pairs={{0,8},{1,9},{2,10},{3,11},{4,12},{5,13},{6,14},{7,15},{8,0},{9,1},... | collective-permute-start | bytes 1253384 | tf_op jit(solution)/shard_map/ppermute | solution.py:168
  27.8 10.4 %collective-permute-start.6 = (bf16[256,768]{1,0:T(8,128)(2,1)S(1)}, bf16[256,768]{1,0:T(8,128)(2,1)S(1)}, u32[]{:S(2)}, u32[]{:S(2)}) collective-permute-start(bf16[256,768]{1,0:T(8,128)(2,1)S(1)} %slice.54), channel_id=1, source_target_pairs={{0,16},{1,17},{2,18},{3,19},{4,20},{5,21},{6,22},{7,23},{8,24},{9,... | collective-permute-start | bytes 1179656 | tf_op jit(solution)/shard_map/ppermute | solution.py:168
  29.4 3.6 %collective-permute-start.4 = (bf16[192,768]{1,0:T(8,128)(2,1)S(1)}, bf16[192,768]{1,0:T(8,128)(2,1)S(1)}, u32[]{:S(2)}, u32[]{:S(2)}) collective-permute-start(bf16[192,768]{1,0:T(8,128)(2,1)S(1)} %slice.53), channel_id=1, source_target_pairs={{0,1},{1,0},{2,3},{3,2},{4,5},{5,4},{6,7},{7,6},{8,9},{9,8},{10,11... | collective-permute-start | bytes 884744 | tf_op jit(solution)/shard_map/ppermute | solution.py:172
  41.3 3.7 %collective-permute-start.9 = (bf16[528,768]{1,0:T(8,128)(2,1)S(1)}, bf16[528,768]{1,0:T(8,128)(2,1)S(1)}, u32[]{:S(2)}, u32[]{:S(2)}) collective-permute-start(bf16[528,768]{1,0:T(8,128)(2,1)S(1)} %collective-permute-done.refs_0_), channel_id=1, source_target_pairs={{0,1},{1,0},{2,3},{3,2},{4,5},{5,4},{6,7},{7,6},{8,9},{9,8},{10,11... | collective-permute-start | bytes 2433032 | tf_op jit(solution)/shard_map/ppermute | solution.py:172
  41.3 12.3 %collective-permute-start.10 = (f32[16,512]{1,0:T(8,128)S(1)}, f32[16,512]{1,0:T(8,128)S(1)}, u32[]{:S(2)}, u32[]{:S(2)}) collective-permute-start(f32[16,512]{1,0:T(8,128)S(1)} %far.1.refs_6_), channel_id=1, source_target_pairs={{0,2},{1,3},{2,4},{3,5},{4,6},{5,7},{6,0},{7,1},{8,10},{9,11},{10,... | collective-permute-start | bytes 98312 | tf_op jit(solution)/shard_map/ppermute | solution.py:178
  47.2 6.4 %collective-permute-start.11 = (f32[2,512]{1,0:T(2,128)S(1)}, f32[2,512]{1,0:T(2,128)S(1)}, u32[]{:S(2)}, u32[]{:S(2)}) collective-permute-start(f32[2,512]{1,0:T(2,128)S(1)} %slice.58), channel_id=1, source_target_pairs={{0,4},{1,5},{2,6},{3,7},{4,0},{5,1},{6,2},{7,3},{8,12},{9,13},{10,... | collective-permute-start | bytes 12296 | tf_op jit(solution)/shard_map/ppermute | solution.py:178
  50.1 4.8 %collective-permute-start.15 = (f32[16,512]{1,0:T(8,128)S(1)}, f32[16,512]{1,0:T(8,128)S(1)}, u32[]{:S(2)}, u32[]{:S(2)}) collective-permute-start(f32[16,512]{1,0:T(8,128)S(1)} %rest.1), channel_id=1, source_target_pairs={{0,24},{1,25},{2,26},{3,27},{4,28},{5,29},{6,30},{7,31},{8,16},{9,... | collective-permute-start | bytes 98312 | tf_op jit(solution)/shard_map/ppermute | solution.py:168
  51.8 3.6 %collective-permute-start.14 = (f32[512]{0:T(512)S(1)}, f32[512]{0:T(512)S(1)}, u32[]{:S(2)}, u32[]{:S(2)}) collective-permute-start(f32[512]{0:T(512)S(1)} %bitcast.14), channel_id=1, source_target_pairs={{0,16},{1,17},{2,18},{3,19},{4,20},{5,21},{6,22},{7,23},{8,24},{9,... | collective-permute-start | bytes 6152 | tf_op jit(solution)/shard_map/ppermute | solution.py:168
  52.3 3.6 %collective-permute-start.13 = (f32[512]{0:T(512)S(1)}, f32[512]{0:T(512)S(1)}, u32[]{:S(2)}, u32[]{:S(2)}) collective-permute-start(f32[512]{0:T(512)S(1)} %bitcast.13), channel_id=1, source_target_pairs={{0,8},{1,9},{2,10},{3,11},{4,12},{5,13},{6,14},{7,15},{8,0},{9,1},... | collective-permute-start | bytes 6152 | tf_op jit(solution)/shard_map/ppermute | solution.py:168
  53.6 2.3 %collective-permute-start.12 = (f32[512]{0:T(512)S(1)}, f32[512]{0:T(512)S(1)}, u32[]{:S(2)}, u32[]{:S(2)}) collective-permute-start(f32[512]{0:T(512)S(1)} %bitcast.15), channel_id=1, source_target_pairs={{0,1},{1,0},{2,3},{3,2},{4,5},{5,4},{6,7},{7,6},{8,9},{9,8},{10,11... | collective-permute-start | bytes 6152 | tf_op jit(solution)/shard_map/ppermute | solution.py:172
